TPU v7x, 32 devices: a whole 2x2x4 slice. The times are simulated.
32 devices in a mesh: dp: 2 (over x), ctx: 16 (over z, y, core).
Axes of the slice: x: 2, y: 2, z: 4, core: 2. Of those that a mesh axis runs over, the one named last changes fastest.
Arguments:
- pre_gate: bfloat16 [2048, 4096], P('dp', 'ctx'), may hold values from -6 to 6
- values: bfloat16 [2048, 4096], P('dp', 'ctx'), may hold values from -6 to 6
- post_gate: bfloat16 [2048, 4096], P('dp', 'ctx'), may hold values from -6 to 6
- filters: float32 [256, 4096], P('ctx', 'dp'), may hold values from -0.09375 to 0.09375
- cotangent: bfloat16 [2048, 4096], P('dp', 'ctx'), may hold values from -6 to 6
Outputs:
- mixed: bfloat16 [2048, 4096], P('dp', 'ctx')
- pre_grad: bfloat16 [2048, 4096], P('dp', 'ctx')
- value_grad: bfloat16 [2048, 4096], P('dp', 'ctx')
- post_grad: bfloat16 [2048, 4096], P('dp', 'ctx')
- filter_grad: float32 [256, 4096], P('ctx', 'dp')
All inputs are finite; a program needn't handle non-finite values.
Results may differ from a plain program's by a relative error of at most 0.014.
Values may be sent and summed in bfloat16 or wider, within the bound.
No kernel may reach another device: no remote copies, remote signals or barrier semaphores. Data moves between devices by JAX's collectives and lax.ppermute only.
A program may use at most 64 MiB of HBM per device.

v0:
```python
import math

import jax
import jax.numpy as jnp
import numpy as np
from jax import lax
from jax.experimental import pallas as pl
from jax.experimental.pallas import tpu as pltpu
from jax.sharding import PartitionSpec as P


LANES = 128
SUBLANES = 8
VMEM_BYTES = 48 * 1024 * 1024


def dft_tables(size):
    angle = np.arange(size)[:, None] * (2.0 * np.arange(size)[None, :] + 1.0) * (math.pi / (2 * size))
    strips = size // LANES
    cos, sin = (part.reshape(size, strips, 1, LANES) for part in (np.cos(angle), np.sin(angle)))
    table = np.concatenate([cos, -sin], axis=2).reshape(size, 2 * size)
    return jnp.asarray(table, jnp.bfloat16), jnp.asarray(table.T / size, jnp.bfloat16)


def dot(left, right):
    return jnp.dot(left, right, preferred_element_type=jnp.float32)


def alternating():
    odd = lax.broadcasted_iota(jnp.int32, (SUBLANES, LANES), 1) % 2
    return 1.0 - 2.0 * odd.astype(jnp.float32)


def place(half_blocks):
    index = lax.axis_index("ctx")
    return index // half_blocks, lax.rem(index, half_blocks)


def real_of(strip):
    return pl.ds(2 * strip * LANES, LANES)


def imag_of(strip):
    return pl.ds((2 * strip + 1) * LANES, LANES)


def gate_kernel(near, half_blocks, pre_ref, value_ref, post_ref, cot_ref, *refs):
    out_refs, (left_ref, right_ref, result_ref, in_sems, out_sems) = refs[:-5], refs[-5:]
    repeats, rows, tokens = left_ref.shape
    share = rows // half_blocks
    half, me = place(half_blocks)
    use_gated = half == 0 if near else half != 0

    def fetch(r, left, right):
        at = pl.ds(r * rows, rows)
        return (
            pltpu.make_async_copy(left.at[at], left_ref.at[r], in_sems.at[0, r]),
            pltpu.make_async_copy(right.at[at], right_ref.at[r], in_sems.at[1, r]),
        )

    @pl.when(use_gated)
    def _():
        for r in range(repeats):
            for copy in fetch(r, pre_ref, value_ref):
                copy.start()

    @pl.when(jnp.logical_not(use_gated))
    def _():
        for r in range(repeats):
            for copy in fetch(r, cot_ref, post_ref):
                copy.start()

    pending = []
    for r in range(repeats):
        for copy in fetch(r, pre_ref, value_ref):
            copy.wait()
        product = left_ref[r].astype(jnp.float32) * right_ref[r].astype(jnp.float32)
        product = product.astype(jnp.bfloat16).reshape(half_blocks, share, tokens)
        if near:
            result_ref[r] = product
            for side in range(2):
                copy = pltpu.make_async_copy(result_ref.at[r], out_refs[0].at[side, :, r], out_sems.at[side, r])
                copy.start()
                pending.append(copy)
        else:
            result_ref[:, r] = product
    if not near:
        even_ref, odd_ref = out_refs
        for at in range(half_blocks // 2):
            slot = slot_order(half_blocks)[at]
            for side, target in ((0, even_ref), (1, odd_ref)):
                source = result_ref.at[jnp.bitwise_xor(me, slot + side)]
                copy = pltpu.make_async_copy(source, target.at[at], out_sems.at[side, at])
                copy.start()
                pending.append(copy)
    for copy in pending:
        copy.wait()


def slot_order(half_blocks):
    return [s for s in range(0, half_blocks, 2) if not s & 2] + [s for s in range(0, half_blocks, 2) if s & 2]


def gate(near, arrays, repeats, half_blocks):
    rows_all, tokens = arrays[0].shape
    rows = rows_all // repeats
    share = rows // half_blocks
    if near:
        shapes = [(2, half_blocks, repeats, share, tokens)]
        held, count = (repeats, half_blocks, share, tokens), repeats
    else:
        shapes = [(half_blocks // 2, repeats, share, tokens)] * 2
        held, count = (half_blocks, repeats, share, tokens), half_blocks // 2
    result = pl.pallas_call(
        lambda *refs: gate_kernel(near, half_blocks, *refs),
        in_specs=[pl.BlockSpec(memory_space=pl.ANY)] * 4,
        out_specs=[pl.BlockSpec(memory_space=pl.ANY)] * len(shapes),
        out_shape=[jax.ShapeDtypeStruct(shape, jnp.bfloat16) for shape in shapes],
        scratch_shapes=[
            pltpu.VMEM((repeats, rows, tokens), jnp.bfloat16),
            pltpu.VMEM((repeats, rows, tokens), jnp.bfloat16),
            pltpu.VMEM(held, jnp.bfloat16),
            pltpu.SemaphoreType.DMA((2, repeats)),
            pltpu.SemaphoreType.DMA((2, count)),
        ],
        compiler_params=pltpu.CompilerParams(vmem_limit_bytes=VMEM_BYTES),
        cost_estimate=pl.CostEstimate(flops=rows_all * tokens, bytes_accessed=8 * rows_all * tokens, transcendentals=0),
        name="gate_near" if near else "gate_own",
    )(*arrays)
    return result[0] if near else result


def finish_kernel(half_blocks, recv_ref, pre_ref, value_ref, post_ref, cot_ref, *refs):
    out_refs, (held_ref, sems) = refs[:4], refs[4:]
    repeats = recv_ref.shape[2]
    rows, tokens = held_ref.shape[2:]
    half, _ = place(half_blocks)
    pending = []
    for r in range(repeats):
        at = pl.ds(r * rows, rows)
        conv = recv_ref[:, half, r].reshape(rows, tokens).astype(jnp.float32)
        grad = recv_ref[:, 1 - half, r].reshape(rows, tokens).astype(jnp.float32)
        for which, (factor_ref, result) in enumerate(
            ((post_ref, conv), (value_ref, grad), (pre_ref, grad), (cot_ref, conv))
        ):
            held_ref[which, r] = (factor_ref[at].astype(jnp.float32) * result).astype(jnp.bfloat16)
            copy = pltpu.make_async_copy(held_ref.at[which, r], out_refs[which].at[at], sems.at[which, r])
            copy.start()
            pending.append(copy)
    for copy in pending:
        copy.wait()


def finish(received, pre_gate, values, post_gate, cotangent):
    half_blocks, _, repeats, share, tokens = received.shape
    rows = half_blocks * share
    return pl.pallas_call(
        lambda *refs: finish_kernel(half_blocks, *refs),
        in_specs=[pl.BlockSpec(memory_space=pltpu.VMEM)] * 5,
        out_specs=[pl.BlockSpec(memory_space=pl.ANY)] * 4,
        out_shape=[jax.ShapeDtypeStruct(pre_gate.shape, jnp.bfloat16)] * 4,
        scratch_shapes=[
            pltpu.VMEM((4, repeats, rows, tokens), jnp.bfloat16),
            pltpu.SemaphoreType.DMA((4, repeats)),
        ],
        compiler_params=pltpu.CompilerParams(vmem_limit_bytes=VMEM_BYTES),
        name="finish",
    )(received, pre_gate, values, post_gate, cotangent)


def taps_kernel(half_blocks, first_ref, second_ref, forward_ref, out_ref, stage_ref):
    count, rows, width = out_ref.shape
    size = width // 2
    share, tokens = first_ref.shape[1:]
    merge = size // tokens
    half, _ = place(half_blocks)
    low, high = first_ref[...], second_ref[...]
    ordered = (jnp.where(half == 0, low, high), jnp.where(half == 0, high, low))
    for part in range(2):
        for k in range(count):
            for q in range(merge):
                stage_ref[k, pl.ds(part * share, share), pl.ds(q * tokens, tokens)] = ordered[part][k * merge + q]
    spectrum = dot(stage_ref[...].reshape(count * rows, size), forward_ref[...]).reshape(count, rows, width)
    turn = jnp.where(half == 0, 1.0, -1.0).astype(jnp.float32)
    sign = alternating()[:1]
    for k in range(count):
        for strip in range(size // LANES):
            re, im = slice(2 * strip * LANES, (2 * strip + 1) * LANES), slice((2 * strip + 1) * LANES, (2 * strip + 2) * LANES)
            real, imag = spectrum[k, :, re], spectrum[k, :, im]
            if k > 0:
                real, imag = real - sign * spectrum[k - 1, :, im], imag + sign * spectrum[k - 1, :, re]
            out_ref[k, :, re] = real
            out_ref[k, :, im] = turn * imag


def transform_taps(first, second, half_blocks, size, forward):
    blocks, share, tokens = first.shape
    count = blocks * tokens // size
    return pl.pallas_call(
        lambda *refs: taps_kernel(half_blocks, *refs),
        out_shape=jax.ShapeDtypeStruct((count, 2 * share, 2 * size), jnp.float32),
        scratch_shapes=[pltpu.VMEM((count, 2 * share, size), jnp.bfloat16)],
        compiler_params=pltpu.CompilerParams(vmem_limit_bytes=VMEM_BYTES),
        name="taps",
    )(first, second, forward)


def exchange_own(even, odd, half_blocks):
    blocks = 2 * half_blocks

    def swap(array, bit):
        return lax.ppermute(array, "ctx", [(i, i ^ bit) for i in range(blocks)])

    order = slot_order(half_blocks)
    groups = [(list(order), even), ([s + 1 for s in order], swap(odd, 1))]
    bit = 2
    while bit < half_blocks:
        kept, leaving, leaving_slots = [], [], []
        for slots, array in groups:
            stays = [at for at, s in enumerate(slots) if not s & bit]
            goes = [at for at, s in enumerate(slots) if s & bit]
            kept.append(([slots[at] for at in stays], take(array, stays)))
            if goes:
                leaving.append(take(array, goes))
                leaving_slots += [slots[at] for at in goes]
        groups = [g for g in kept if g[0]] + [(leaving_slots, swap(jnp.concatenate(leaving), bit))]
        bit *= 2
    return groups


def take(array, rows):
    if not rows:
        return None
    if rows == list(range(rows[0], rows[0] + len(rows))):
        return array[rows[0] : rows[0] + len(rows)]
    return jnp.concatenate([array[at : at + 1] for at in rows])


def add(total, term):
    return term if total is None else (total[0] + term[0], total[1] + term[1])


def times(a, b):
    return a[0] * b[0] - a[1] * b[1], a[0] * b[1] + a[1] * b[0]


def conj_times(a, b):
    return a[0] * b[0] + a[1] * b[1], a[0] * b[1] - a[1] * b[0]


def convolve_kernel(half_blocks, slots, near_ref, *refs):
    own_refs = refs[: len(slots)]
    filt_ref, forward_ref, inverse_ref, out_ref, stage_ref, spec_ref, prod_ref = refs[len(slots) :]
    _, count, rows, width = spec_ref.shape
    size = width // 2
    tokens = near_ref.shape[2]
    merge = size // tokens
    filters = filt_ref.shape[1]
    half, _ = place(half_blocks)
    fill_stage(half_blocks, merge, near_ref, own_refs, slots, stage_ref)
    spec_ref[...] = dot(stage_ref[...].reshape(3 * count * rows, size), forward_ref[...]).reshape(spec_ref.shape)

    @pl.loop(0, rows // SUBLANES)
    def _(tile):
        row = pl.ds(pl.multiple_of(tile * SUBLANES, SUBLANES), SUBLANES)
        tap_row = pl.ds(pl.multiple_of(lax.rem(tile * SUBLANES, filters), SUBLANES), SUBLANES)
        for strip in range(size // LANES):
            def spectrum(which, k):
                return spec_ref[which, k, row, real_of(strip)], spec_ref[which, k, row, imag_of(strip)]

            taps = [
                (filt_ref[k, tap_row, real_of(strip)], filt_ref[k, tap_row, imag_of(strip)]) for k in range(2 * count)
            ]
            near = [spectrum(0, k) for k in range(count)]
            for out in range(count):
                total = None
                for k in range(out + 1):
                    total = add(total, times(taps[out - k], near[k]))
                prod_ref[0, out, row, real_of(strip)], prod_ref[0, out, row, imag_of(strip)] = total
            own = [spectrum(1, k) for k in range(count)]
            far = [spectrum(2, k) for k in range(count)]
            for out in range(count):
                total = None
                for k in range(out + 1):
                    total = add(total, conj_times(taps[out - k], own[k]))
                for k in range(count):
                    total = add(total, conj_times(taps[count + out - k], far[k]))
                prod_ref[1, out, row, real_of(strip)], prod_ref[1, out, row, imag_of(strip)] = total

    result = dot(prod_ref[...].astype(jnp.bfloat16).reshape(2 * count * rows, width), inverse_ref[...])
    result = result.astype(jnp.bfloat16).reshape(2, count, rows, size)
    for k in range(count):
        flipped = count - 1 - k
        outer = jnp.where(half == 0, k, flipped)
        inner = jnp.where(half == 0, flipped, k)
        for q in range(merge):
            lanes = slice(q * tokens, (q + 1) * tokens)
            out_ref[outer * merge + q, 0] = result[0, k, :, lanes]
            out_ref[inner * merge + q, 1] = result[1, k, :, lanes]


def fill_stage(half_blocks, merge, near_ref, own_refs, slots, stage_ref):
    count = half_blocks // merge
    tokens = near_ref.shape[2]
    half, me = place(half_blocks)
    for k in range(count):
        flipped = count - 1 - k
        outer = jnp.where(half == 0, k, flipped)
        inner = jnp.where(half == 0, flipped, k)
        for q in range(merge):
            lanes = pl.ds(q * tokens, tokens)
            stage_ref[0, k, :, lanes] = near_ref[half * half_blocks + outer * merge + q]
            stage_ref[2, k, :, lanes] = near_ref[(1 - half) * half_blocks + inner * merge + q]
    for group, ref in zip(slots, own_refs):
        for at, slot in enumerate(group):
            position = jnp.bitwise_xor(me, slot)
            block = position // merge
            k = jnp.where(half == 0, count - 1 - block, block)
            start = pl.multiple_of(lax.rem(position, merge) * tokens, tokens)
            stage_ref[1, k, :, pl.ds(start, tokens)] = ref[at]


def convolve(near, own, filt, half_blocks, tables):
    forward, inverse = tables
    _, rows, tokens = near.shape
    size = forward.shape[0]
    count = half_blocks * tokens // size
    slots = [group for group, _ in own]
    pairs = count * (2 * count + 1)
    return pl.pallas_call(
        lambda *refs: convolve_kernel(half_blocks, slots, *refs),
        out_shape=jax.ShapeDtypeStruct((half_blocks, 2, rows, tokens), jnp.bfloat16),
        scratch_shapes=[
            pltpu.VMEM((3, count, rows, size), jnp.bfloat16),
            pltpu.VMEM((3, count, rows, 2 * size), jnp.float32),
            pltpu.VMEM((2, count, rows, 2 * size), jnp.float32),
        ],
        compiler_params=pltpu.CompilerParams(vmem_limit_bytes=VMEM_BYTES),
        cost_estimate=pl.CostEstimate(
            flops=20 * count * rows * size * size + 8 * pairs * rows * size,
            bytes_accessed=10 * count * rows * size,
            transcendentals=0,
        ),
        name="convolve",
    )(near, *[array for _, array in own], filt, forward, inverse)


def correlate_kernel(half_blocks, slots, near_ref, *refs):
    own_refs = refs[: len(slots)]
    forward_ref, inverse_ref, keep_ref, give_ref, stage_ref, spec_ref, local_ref, cross_ref, joint_ref = refs[len(slots) :]
    _, count, rows, width = spec_ref.shape
    size = width // 2
    tokens = near_ref.shape[2]
    merge = size // tokens
    filters = local_ref.shape[1]
    repeats = rows // filters
    kept = filters // 2
    half, _ = place(half_blocks)
    turn = jnp.where(half == 0, 1.0, -1.0).astype(jnp.float32)
    fill_stage(half_blocks, merge, near_ref, own_refs, slots, stage_ref)
    spec_ref[...] = dot(stage_ref[...].reshape(3 * count * rows, size), forward_ref[...]).reshape(spec_ref.shape)

    def products(other, row_at, strip, lags):
        totals = [None] * len(lags)
        for repeat in range(repeats):
            row = pl.ds(pl.multiple_of(repeat * filters + row_at, SUBLANES), SUBLANES)

            def spectrum(which, k):
                return spec_ref[which, k, row, real_of(strip)], spec_ref[which, k, row, imag_of(strip)]

            near = [spectrum(0, k) for k in range(count)]
            far = [spectrum(other, k) for k in range(count)]
            for at, total in enumerate(lags):
                for a in range(count):
                    if 0 <= total - a < count:
                        totals[at] = add(totals[at], conj_times(near[a], far[total - a]))
        return totals

    @pl.loop(0, filters // SUBLANES)
    def _(tile):
        row = pl.multiple_of(tile * SUBLANES, SUBLANES)
        for strip in range(size // LANES):
            totals = products(1, row, strip, [count - 1 - k for k in range(count)])
            for k in range(count):
                local_ref[k, pl.ds(row, SUBLANES), real_of(strip)] = totals[k][0]
                local_ref[k, pl.ds(row, SUBLANES), imag_of(strip)] = turn * totals[k][1]

    @pl.loop(0, kept // SUBLANES)
    def _(tile):
        to = pl.multiple_of(tile * SUBLANES, SUBLANES)
        row = pl.multiple_of(half * kept + tile * SUBLANES, SUBLANES)
        for strip in range(size // LANES):
            totals = products(2, row, strip, [2 * count - 1 - k for k in range(1, 2 * count)])
            for k in range(1, 2 * count):
                real, imag = totals[k - 1]
                imag = turn * imag
                if k < count:
                    real = real + local_ref[k, pl.ds(row, SUBLANES), real_of(strip)]
                    imag = imag + local_ref[k, pl.ds(row, SUBLANES), imag_of(strip)]
                cross_ref[k, pl.ds(to, SUBLANES), real_of(strip)] = real
                cross_ref[k, pl.ds(to, SUBLANES), imag_of(strip)] = imag
            cross_ref[0, pl.ds(to, SUBLANES), real_of(strip)] = local_ref[0, pl.ds(row, SUBLANES), real_of(strip)]
            cross_ref[0, pl.ds(to, SUBLANES), imag_of(strip)] = local_ref[0, pl.ds(row, SUBLANES), imag_of(strip)]

    sign = alternating()[:1]
    other = pl.ds(pl.multiple_of((1 - half) * kept, SUBLANES), kept)

    def join(ref, row, lags, base):
        for k in range(lags):
            for strip in range(size // LANES):
                real, imag = ref[k, row, real_of(strip)], ref[k, row, imag_of(strip)]
                if k + 1 < lags:
                    real, imag = (
                        real + sign * ref[k + 1, row, imag_of(strip)],
                        imag - sign * ref[k + 1, row, real_of(strip)],
                    )
                joint_ref[base + k, :, real_of(strip)] = real.astype(jnp.bfloat16)
                joint_ref[base + k, :, imag_of(strip)] = imag.astype(jnp.bfloat16)

    join(cross_ref, pl.ds(0, kept), 2 * count, 0)
    join(local_ref, other, count, 2 * count)
    result = dot(joint_ref[...].reshape(3 * count * kept, width), inverse_ref[...]).reshape(3 * count, kept, size)
    for k in range(3 * count):
        for q in range(merge):
            piece = result[k, :, q * tokens : (q + 1) * tokens]
            if k < 2 * count:
                keep_ref[k * merge + q] = piece
            else:
                give_ref[(k - 2 * count) * merge + q] = piece.astype(jnp.bfloat16)


def correlate(near, own, filters, half_blocks, tables):
    forward, inverse = tables
    _, rows, tokens = near.shape
    size = forward.shape[0]
    count = half_blocks * tokens // size
    slots = [group for group, _ in own]
    pairs = count * (2 * count + 1)
    kept = filters // 2
    return pl.pallas_call(
        lambda *refs: correlate_kernel(half_blocks, slots, *refs),
        out_shape=[
            jax.ShapeDtypeStruct((2 * half_blocks, kept, tokens), jnp.float32),
            jax.ShapeDtypeStruct((half_blocks, kept, tokens), jnp.bfloat16),
        ],
        scratch_shapes=[
            pltpu.VMEM((3, count, rows, size), jnp.bfloat16),
            pltpu.VMEM((3, count, rows, 2 * size), jnp.float32),
            pltpu.VMEM((count, filters, 2 * size), jnp.float32),
            pltpu.VMEM((2 * count, kept, 2 * size), jnp.float32),
            pltpu.VMEM((3 * count, kept, 2 * size), jnp.bfloat16),
        ],
        compiler_params=pltpu.CompilerParams(vmem_limit_bytes=VMEM_BYTES),
        cost_estimate=pl.CostEstimate(
            flops=14 * count * rows * size * size + 4 * pairs * rows * size,
            bytes_accessed=8 * count * rows * size,
            transcendentals=0,
        ),
        name="correlate",
    )(near, *[array for _, array in own], forward, inverse)


def body(pre_gate, values, post_gate, filters, cotangent):
    blocks = lax.axis_size("ctx")
    groups = lax.axis_size("dp")
    half_blocks = blocks // 2
    local_rows, tokens = pre_gate.shape
    local_filters = filters.shape[0]
    repeats = local_rows // (local_filters * blocks)
    owned = 2 * local_filters
    lags = blocks // groups
    tables = dft_tables(2 * tokens)
    group = lax.axis_index("dp")
    half = lax.axis_index("ctx") // half_blocks
    arrays = (pre_gate, values, post_gate, cotangent)

    near = gate(True, arrays, repeats, half_blocks)
    near = lax.all_to_all(
        near.reshape(blocks, repeats * owned, tokens), "ctx", split_axis=0, concat_axis=0, tiled=True
    )

    tap_local = jnp.transpose(filters.reshape(local_filters, lags, tokens), (1, 0, 2)).astype(jnp.bfloat16)
    tap_other = lax.ppermute(tap_local, "dp", [(0, 1), (1, 0)])
    tap_all = jnp.where(
        group == 0,
        jnp.concatenate([tap_local, tap_other]),
        jnp.concatenate([tap_other, tap_local]),
    )
    first = lax.ppermute(tap_all, "ctx", [(i, i // 2 + (i % 2) * half_blocks) for i in range(blocks)])
    second = lax.ppermute(tap_all, "ctx", [(i, i // 2 + (1 - i % 2) * half_blocks) for i in range(blocks)])
    filt = transform_taps(first, second, half_blocks, 2 * tokens, tables[0])

    even, odd = gate(False, arrays, repeats, half_blocks)
    shape = (half_blocks // 2, repeats * owned, tokens)
    own = exchange_own(even.reshape(shape), odd.reshape(shape), half_blocks)

    result = convolve(near, own, filt, half_blocks, tables)
    sides = [list(range(half_blocks)), list(range(half_blocks, blocks))]
    returned = lax.all_to_all(
        result, "ctx", split_axis=0, concat_axis=0, tiled=True, axis_index_groups=sides
    )

    keep, give = correlate(near, own, owned, half_blocks, tables)
    taken = lax.ppermute(give, "ctx", [(i, (i + half_blocks) % blocks) for i in range(blocks)])
    low = keep[:half_blocks] + taken.astype(jnp.float32)
    high = keep[half_blocks:]
    mine = jnp.where(group == 0, low, high).astype(jnp.bfloat16)
    theirs = jnp.where(group == 0, high, low).astype(jnp.bfloat16)
    home = [(i, 2 * (i % half_blocks) + i // half_blocks) for i in range(blocks)]
    mine = lax.ppermute(mine, "ctx", home)
    theirs = lax.ppermute(
        theirs, ("dp", "ctx"), [(g * blocks + i, (1 - g) * blocks + j) for g in range(groups) for i, j in home]
    )
    summed = mine.astype(jnp.float32) + theirs.astype(jnp.float32)
    filter_grad = jnp.transpose(summed, (1, 0, 2)).reshape(local_filters, lags * tokens)

    returned = returned.reshape(half_blocks, 2, repeats, owned, tokens)
    mixed, pre_grad, value_grad, post_grad = finish(returned, pre_gate, values, post_gate, cotangent)
    return (mixed, pre_grad, value_grad, post_grad, filter_grad)


def matmul(left, right):
    return jnp.dot(left, right, precision=lax.Precision.HIGHEST, preferred_element_type=jnp.float32)


def contract(form, left, right):
    return jnp.einsum(
        form, left, right, precision=lax.Precision.HIGHEST, preferred_element_type=jnp.float32
    )


def phases(height, width, modulus):
    product = lax.broadcasted_iota(jnp.int32, (height, width), 0) * lax.broadcasted_iota(
        jnp.int32, (height, width), 1
    )
    return (product % modulus).astype(jnp.float32) * (2.0 * math.pi / modulus)


def build_tables(blocks, tokens):
    factor = 1
    for candidate in range(1, tokens + 1):
        if tokens % candidate == 0 and candidate * candidate <= tokens:
            factor = candidate
    second = tokens // factor
    rows = blocks + 1
    total = 2 * blocks * tokens
    first_angle = phases(rows, blocks, 2 * blocks)
    twist_angle = phases(rows, tokens, total)
    inner_angle = phases(factor, factor, factor)
    middle_angle = phases(factor, second, tokens)
    outer_angle = phases(second, second, second)
    back_angle = phases(blocks, rows, 2 * blocks)
    column = lax.broadcasted_iota(jnp.int32, (blocks, rows), 1)
    weight = jnp.where((column == 0) | (column == blocks), 1.0, 2.0).astype(jnp.float32) / total
    return {
        "first_cos": jnp.cos(first_angle),
        "first_nsin": -jnp.sin(first_angle),
        "twist_cos": jnp.cos(twist_angle),
        "twist_sin": jnp.sin(twist_angle),
        "inner_cos": jnp.cos(inner_angle),
        "inner_sin": jnp.sin(inner_angle),
        "middle_cos": jnp.cos(middle_angle),
        "middle_sin": jnp.sin(middle_angle),
        "outer_cos": jnp.cos(outer_angle),
        "outer_sin": jnp.sin(outer_angle),
        "back_cos": weight * jnp.cos(back_angle),
        "back_sin": weight * jnp.sin(back_angle),
    }


def expand(table, ndim):
    return table.reshape((table.shape[0],) + (1,) * (ndim - 2) + (table.shape[1],))


def block_table(cos_part, sin_part):
    return jnp.stack([jnp.stack([cos_part, sin_part]), jnp.stack([-sin_part, cos_part])])


def wave(real_part, imag_part, tables, sign):
    shape = real_part.shape
    factor = tables["inner_cos"].shape[0]
    second = tables["outer_cos"].shape[0]
    stacked = jnp.stack(
        [real_part.reshape(-1, factor, second), imag_part.reshape(-1, factor, second)]
    )
    inner_table = block_table(tables["inner_cos"], sign * tables["inner_sin"])
    middle = contract("prab,pqac->qrcb", stacked, inner_table)
    middle_cos = tables["middle_cos"]
    middle_sin = sign * tables["middle_sin"]
    real_turn = middle[0] * middle_cos - middle[1] * middle_sin
    imag_turn = middle[0] * middle_sin + middle[1] * middle_cos
    turned = jnp.stack([real_turn, imag_turn])
    outer_table = block_table(tables["outer_cos"], sign * tables["outer_sin"])
    result = contract("prcb,pqbd->qrdc", turned, outer_table)
    return (result[0].reshape(shape), result[1].reshape(shape))


def finish_forward(real_first, imag_first, tables):
    ndim = real_first.ndim
    twist_cos = expand(tables["twist_cos"], ndim)
    twist_sin = expand(tables["twist_sin"], ndim)
    real_twist = real_first * twist_cos + imag_first * twist_sin
    imag_twist = imag_first * twist_cos - real_first * twist_sin
    return wave(real_twist, imag_twist, tables, -1.0)


def spectrum(signal, tables):
    flat = signal.reshape(signal.shape[0], -1)
    shape = (tables["first_cos"].shape[0],) + signal.shape[1:]
    real_first = matmul(tables["first_cos"], flat).reshape(shape)
    imag_first = matmul(tables["first_nsin"], flat).reshape(shape)
    return finish_forward(real_first, imag_first, tables)


def inverse_prepare(real_spec, imag_spec, tables):
    ndim = real_spec.ndim
    real_wave, imag_wave = wave(real_spec, imag_spec, tables, 1.0)
    twist_cos = expand(tables["twist_cos"], ndim)
    twist_sin = expand(tables["twist_sin"], ndim)
    real_twist = real_wave * twist_cos - imag_wave * twist_sin
    imag_twist = real_wave * twist_sin + imag_wave * twist_cos
    rows = real_spec.shape[0]
    return (real_twist.reshape(rows, -1), imag_twist.reshape(rows, -1))


def inverse_full(real_spec, imag_spec, tables):
    real_flat, imag_flat = inverse_prepare(real_spec, imag_spec, tables)
    signal = matmul(tables["back_cos"], real_flat) - matmul(tables["back_sin"], imag_flat)
    return signal.reshape((tables["back_cos"].shape[0],) + real_spec.shape[1:])


def plain_body(pre_gate, values, post_gate, filters, cotangent):
    blocks = lax.axis_size("ctx")
    groups = lax.axis_size("dp")
    local_rows = pre_gate.shape[0]
    tokens = pre_gate.shape[1]
    local_filters = filters.shape[0]
    repeats = local_rows // (local_filters * blocks)
    share = blocks // groups
    tables = build_tables(blocks, tokens)
    gated = (pre_gate.astype(jnp.float32) * values.astype(jnp.float32)).astype(jnp.bfloat16)
    conv_grad = (cotangent.astype(jnp.float32) * post_gate.astype(jnp.float32)).astype(jnp.bfloat16)
    gated_blocks = gated.reshape(repeats, blocks, local_filters, tokens)
    grad_blocks = conv_grad.reshape(repeats, blocks, local_filters, tokens)
    tap_local = jnp.transpose(filters.reshape(local_filters, share, tokens), (1, 0, 2))
    piece = lax.all_gather(tap_local, "dp", axis=0, tiled=True)
    count = piece.shape[0]
    flat = piece.reshape(count, -1)
    cos_cols = tables["first_cos"]
    sin_cols = tables["first_nsin"]
    real_first = matmul(cos_cols, flat)
    imag_first = matmul(sin_cols, flat)
    spec_shape = (blocks + 1, 1, local_filters, tokens)
    filt_real, filt_imag = finish_forward(
        real_first.reshape(spec_shape), imag_first.reshape(spec_shape), tables
    )

    def single_spectrum(received):
        signal = received.reshape(blocks, -1, received.shape[2], received.shape[3])
        return spectrum(signal.astype(jnp.float32), tables)

    gated_real, gated_imag = single_spectrum(
        lax.all_to_all(gated_blocks, "ctx", split_axis=1, concat_axis=0, tiled=True)
    )
    prod_real = gated_real * filt_real - gated_imag * filt_imag
    prod_imag = gated_real * filt_imag + gated_imag * filt_real
    result = inverse_full(prod_real, prod_imag, tables).astype(jnp.bfloat16)
    conv_chan = result.reshape(blocks * repeats, 1, local_filters, tokens)
    conv_seq = lax.all_to_all(conv_chan, "ctx", split_axis=0, concat_axis=1, tiled=True)
    grad_real, grad_imag = single_spectrum(
        lax.all_to_all(grad_blocks, "ctx", split_axis=1, concat_axis=0, tiled=True)
    )
    prod_real = filt_real * grad_real + filt_imag * grad_imag
    prod_imag = filt_real * grad_imag - filt_imag * grad_real
    result = inverse_full(prod_real, prod_imag, tables).astype(jnp.bfloat16)
    gated_chan_grad = result.reshape(blocks * repeats, 1, local_filters, tokens)
    gated_seq_grad = lax.all_to_all(gated_chan_grad, "ctx", split_axis=0, concat_axis=1, tiled=True)
    cross_real = jnp.sum(gated_real * grad_real + gated_imag * grad_imag, axis=1)
    cross_imag = jnp.sum(gated_real * grad_imag - gated_imag * grad_real, axis=1)
    wave_real, wave_imag = inverse_prepare(cross_real, cross_imag, tables)
    cos_rows = tables["back_cos"]
    sin_rows = tables["back_sin"]
    term = matmul(cos_rows, wave_real) - matmul(sin_rows, wave_imag)
    summed = lax.psum_scatter(
        term.reshape(lax.axis_size("dp") * share, local_filters, tokens).astype(jnp.bfloat16),
        "dp",
        scatter_dimension=0,
        tiled=True,
    ).astype(jnp.float32)
    filter_grad = jnp.transpose(summed, (1, 0, 2)).reshape(local_filters, share * tokens)
    conv_full = conv_seq.reshape(pre_gate.shape).astype(jnp.float32)
    gated_grad = gated_seq_grad.reshape(pre_gate.shape).astype(jnp.float32)
    mixed = (post_gate.astype(jnp.float32) * conv_full).astype(jnp.bfloat16)
    post_grad = (cotangent.astype(jnp.float32) * conv_full).astype(jnp.bfloat16)
    pre_grad = (gated_grad * values.astype(jnp.float32)).astype(jnp.bfloat16)
    value_grad = (gated_grad * pre_gate.astype(jnp.float32)).astype(jnp.bfloat16)
    return (mixed, pre_grad, value_grad, post_grad, filter_grad)


def solution(mesh):
    placed = (P("dp", "ctx"), P("dp", "ctx"), P("dp", "ctx"), P("ctx", "dp"), P("dp", "ctx"))
    groups, blocks = mesh.shape["dp"], mesh.shape["ctx"]

    def program(pre_gate, values, post_gate, filters, cotangent):
        kernels = groups == 2 and blocks >= 8 and blocks & (blocks - 1) == 0 and filters.shape[0] % 16 == 0
        return (body if kernels else plain_body)(pre_gate, values, post_gate, filters, cotangent)

    return jax.shard_map(
        program,
        mesh=mesh,
        in_specs=placed,
        out_specs=(P("dp", "ctx"), P("dp", "ctx"), P("dp", "ctx"), P("dp", "ctx"), P("ctx", "dp")),
        check_vma=False,
    )
```

profile of v0, /device:TPU:8, one launch (start us, length us, event | category | flops | bytes accessed | tf_op | source)
XLA Modules:
  0.0 91.8 jit_solution(11126944435169790403)
XLA Ops:
  2.7 1.0 %copy-done.4 = bf16[1024,256]{1,0:T(8,128)(2,1)S(1)} copy-done((bf16[1024,256]{1,0:T(8,128)(2,1)S(1)}, bf16[1024,256]{1,0:T(8,128)(2,1)}, u32[]{:S(2)}) %copy-start.4) | copy-done | bytes 524312
  3.8 1.0 %copy-done.6 = bf16[1024,256]{1,0:T(8,128)(2,1)S(1)} copy-done((bf16[1024,256]{1,0:T(8,128)(2,1)S(1)}, bf16[1024,256]{1,0:T(8,128)(2,1)}, u32[]{:S(2)}) %copy-start.6) | copy-done | bytes 524312
  4.8 2.5 %gate_near.1 = bf16[2,8,4,32,256]{4,3,2,1,0:T(8,128)(2,1)} custom-call(bf16[1024,256]{1,0:T(8,128)(2,1)S(1)} %copy-done, bf16[1024,256]{1,0:T(8,128)(2,1)S(1)} %copy-done.2, bf16[1024,256]{1,0:T(8,128)(2,1)S(1)} %copy-done.4, bf16[1024,256]{1,0:T(8,128)(2,1)S(1)} %copy-done.6), custom_call_target="tpu_custom_call" | custom-call | flops 262144 | bytes 2097152 | tf_op jit(solution)/shard_map/gate_near/pallas_call | solution.py:114
  7.4 6.4 %all-to-all-start = ((bf16[16,128,256]{2,1,0:T(8,128)(2,1)}), bf16[16,128,256]{2,1,0:T(8,128)(2,1)}, u32[]{:S(2)}, u32[]{:S(2)}) async-start(bf16[16,128,256]{2,1,0:T(8,128)(2,1)} %bitcast), calls=%async_computation | async-start | bytes 2097152 | tf_op jit(solution)/shard_map/all_to_all | solution.py:478
  13.8 2.3 %gate_own.1 = (bf16[4,4,32,256]{3,2,1,0:T(8,128)(2,1)S(1)}, bf16[4,4,32,256]{3,2,1,0:T(8,128)(2,1)S(1)}) custom-call(bf16[1024,256]{1,0:T(8,128)(2,1)S(1)} %copy-done.1, bf16[1024,256]{1,0:T(8,128)(2,1)S(1)} %copy-done.3, bf16[1024,256]{1,0:T(8,128)(2,1)S(1)} %copy-done.5, bf16[1024,256]{1,0:T(8,128)(2,1)S(1)} %copy-done.7), custom_call_target="tpu_custom_call" | custom-call | flops 262144 | bytes 2097152 | tf_op jit(solution)/shard_map/gate_own/pallas_call | solution.py:114
  17.1 1.5 %collective-permute-start.3 = (bf16[8,16,256]{2,1,0:T(8,128)(2,1)}, bf16[8,16,256]{2,1,0:T(8,128)(2,1)}, u32[]{:S(2)}, u32[]{:S(2)}) collective-permute-start(bf16[8,16,256]{2,1,0:T(8,128)(2,1)} %bitcast.16), channel_id=1, source_target_pairs={{0,16},{16,0},{1,17},{17,1},{2,18},{18,2},{3,19},{19,3},{4,20},{20... | collective-permute-start | bytes 196616 | tf_op jit(solution)/shard_map/ppermute | solution.py:483
  19.3 1.5 %collective-permute-start.1 = (bf16[4,128,256]{2,1,0:T(8,128)(2,1)}, bf16[4,128,256]{2,1,0:T(8,128)(2,1)}, u32[]{:S(2)}, u32[]{:S(2)}) collective-permute-start(bf16[4,128,256]{2,1,0:T(8,128)(2,1)} %pad_maximum_fusion), channel_id=1, source_target_pairs={{0,2},{1,3},{2,0},{3,1},{4,6},{5,7},{6,4},{7,5},{8,10},{9,11},{10,... | collective-permute-start | bytes 786440 | tf_op jit(solution)/shard_map/ppermute | solution.py:212
  21.5 11.6 %collective-permute-done.1 = bf16[4,128,256]{2,1,0:T(8,128)(2,1)} collective-permute-done((bf16[4,128,256]{2,1,0:T(8,128)(2,1)}, bf16[4,128,256]{2,1,0:T(8,128)(2,1)}, u32[]{:S(2)}, u32[]{:S(2)}) %collective-permute-start.1) | collective-permute-done | bytes 262176 | tf_op jit(solution)/shard_map/ppermute | solution.py:212
  35.9 1.6 %collective-permute-start.5 = (bf16[16,16,256]{2,1,0:T(8,128)(2,1)S(1)}, bf16[16,16,256]{2,1,0:T(8,128)(2,1)S(1)}, u32[]{:S(2)}, u32[]{:S(2)}) collective-permute-start(bf16[16,16,256]{2,1,0:T(8,128)(2,1)S(1)} %maximum_select_fusion), channel_id=1, source_target_pairs={{0,8},{1,0},{2,9},{3,1},{4,10},{5,2},{6,11},{7,3},{8,12},{9,4},{10... | collective-permute-start | bytes 393224 | tf_op jit(solution)/shard_map/ppermute | solution.py:490
  37.5 3.6 %collective-permute-start.4 = (bf16[16,16,256]{2,1,0:T(8,128)(2,1)S(1)}, bf16[16,16,256]{2,1,0:T(8,128)(2,1)S(1)}, u32[]{:S(2)}, u32[]{:S(2)}) collective-permute-start(bf16[16,16,256]{2,1,0:T(8,128)(2,1)S(1)} %maximum_select_fusion), channel_id=1, source_target_pairs={{0,0},{1,8},{2,1},{3,9},{4,2},{5,10},{6,3},{7,11},{8,4},{9,12},{10... | collective-permute-start | bytes 393224 | tf_op jit(solution)/shard_map/ppermute | solution.py:489
  41.0 5.3 %collective-permute-done.4.refs_0_ = bf16[16,16,256]{2,1,0:T(8,128)(2,1)S(1)} collective-permute-done((bf16[16,16,256]{2,1,0:T(8,128)(2,1)S(1)}, bf16[16,16,256]{2,1,0:T(8,128)(2,1)S(1)}, u32[]{:S(2)}, u32[]{:S(2)}) %collective-permute-start.4) | collective-permute-done | bytes 131104 | tf_op jit(solution)/shard_map/ppermute | solution.py:489
  48.5 1.2 %copy-done.12 = f32[8,32,1024]{2,1,0:T(8,128)S(1)} copy-done((f32[8,32,1024]{2,1,0:T(8,128)S(1)}, f32[8,32,1024]{2,1,0:T(8,128)}, u32[]{:S(2)}) %copy-start.12) | copy-done | bytes 1048600
  50.7 1.2 %copy-done.16 = bf16[1024,512]{1,0:T(8,128)(2,1)S(1)} copy-done((bf16[1024,512]{1,0:T(8,128)(2,1)S(1)}, bf16[1024,512]{1,0:T(8,128)(2,1)}, u32[]{:S(2)}) %copy-start.16) | copy-done | bytes 1048600
  51.9 6.8 %convolve.1 = bf16[8,2,128,256]{3,2,1,0:T(8,128)(2,1)S(1)} custom-call(bf16[16,128,256]{2,1,0:T(8,128)(2,1)} %all-to-all-done.refs_0_, bf16[1,128,256]{2,1,0:T(8,128)(2,1)S(1)} %bitcast.18, bf16[1,128,256]{2,1,0:T(8,128)(2,1)S(1)} %get-tuple-element.26.refs_2_, bf16[2,128,256]{2,1,0:T(8,128)(2,1)S(1)} %pad_maximum_fusion.2.refs_3_, ...), custom_call_target="tpu_custom_call" | custom-call | flops 2703228928 | bytes 2621440 | tf_op jit(solution)/shard_map/convolve/pallas_call | solution.py:330
  59.7 3.5 %all-to-all-start.1 = ((bf16[8,2,128,256]{3,2,1,0:T(8,128)(2,1)}), bf16[8,2,128,256]{3,2,1,0:T(8,128)(2,1)S(1)}, u32[]{:S(2)}, u32[]{:S(2)}) async-start(bf16[8,2,128,256]{3,2,1,0:T(8,128)(2,1)} %copy-done.10), calls=%async_computation.1 | async-start | bytes 2097152 | tf_op jit(solution)/shard_map/all_to_all | solution.py:499
  63.2 1.2 %copy-done.9 = bf16[512,1024]{1,0:T(8,128)(2,1)S(1)} copy-done((bf16[512,1024]{1,0:T(8,128)(2,1)S(1)}, bf16[512,1024]{1,0:T(8,128)(2,1)}, u32[]{:S(2)}) %copy-start.9) | copy-done | bytes 1048600
  65.4 1.2 %copy-done.17 = bf16[1024,512]{1,0:T(8,128)(2,1)S(1)} copy-done((bf16[1024,512]{1,0:T(8,128)(2,1)S(1)}, bf16[1024,512]{1,0:T(8,128)(2,1)}, u32[]{:S(2)}) %copy-start.17) | copy-done | bytes 1048600
  66.6 4.8 %correlate.1 = (f32[16,16,256]{2,1,0:T(8,128)S(1)}, bf16[8,16,256]{2,1,0:T(8,128)(2,1)S(1)}) custom-call(bf16[16,128,256]{2,1,0:T(8,128)(2,1)} %all-to-all-done.refs_0_, bf16[1,128,256]{2,1,0:T(8,128)(2,1)S(1)} %bitcast.19, bf16[1,128,256]{2,1,0:T(8,128)(2,1)S(1)} %get-tuple-element.26.refs_2_, bf16[2,128,256]{2,1,0:T(8,128)(2,1)S(1)} %pad_maximum_fusion.2.refs_3_, ...), custom_call_target="tpu_custom_call" | custom-call | flops 1888485376 | bytes 2097152 | tf_op jit(solution)/shard_map/correlate/pallas_call | solution.py:440
  71.5 2.6 %collective-permute-start.6 = (bf16[8,16,256]{2,1,0:T(8,128)(2,1)S(1)}, bf16[8,16,256]{2,1,0:T(8,128)(2,1)S(1)}, u32[]{:S(2)}, u32[]{:S(2)}) collective-permute-start(bf16[8,16,256]{2,1,0:T(8,128)(2,1)S(1)} %get-tuple-element.20), channel_id=1, source_target_pairs={{0,8},{1,9},{2,10},{3,11},{4,12},{5,13},{6,14},{7,15},{8,0},{9,1},... | collective-permute-start | bytes 196616 | tf_op jit(solution)/shard_map/ppermute | solution.py:504
  74.1 5.3 %collective-permute-done.6 = bf16[8,16,256]{2,1,0:T(8,128)(2,1)S(1)} collective-permute-done((bf16[8,16,256]{2,1,0:T(8,128)(2,1)S(1)}, bf16[8,16,256]{2,1,0:T(8,128)(2,1)S(1)}, u32[]{:S(2)}, u32[]{:S(2)}) %collective-permute-start.6) | collective-permute-done | bytes 65568 | tf_op jit(solution)/shard_map/ppermute | solution.py:504
  79.4 1.9 %collective-permute-start.7 = (bf16[8,16,256]{2,1,0:T(8,128)(2,1)S(1)}, bf16[8,16,256]{2,1,0:T(8,128)(2,1)S(1)}, u32[]{:S(2)}, u32[]{:S(2)}) collective-permute-start(bf16[8,16,256]{2,1,0:T(8,128)(2,1)S(1)} %get-tuple-element.21), channel_id=1, source_target_pairs={{0,0},{1,2},{2,4},{3,6},{4,8},{5,10},{6,12},{7,14},{8,1},{9,3},{10... | collective-permute-start | bytes 196616 | tf_op jit(solution)/shard_map/ppermute | solution.py:510
  81.9 4.7 %collective-permute-done.7 = bf16[8,16,256]{2,1,0:T(8,128)(2,1)S(1)} collective-permute-done((bf16[8,16,256]{2,1,0:T(8,128)(2,1)S(1)}, bf16[8,16,256]{2,1,0:T(8,128)(2,1)S(1)}, u32[]{:S(2)}, u32[]{:S(2)}) %collective-permute-start.7) | collective-permute-done | bytes 65568 | tf_op jit(solution)/shard_map/ppermute | solution.py:510
  86.6 3.0 %collective-permute-done.8 = bf16[8,16,256]{2,1,0:T(8,128)(2,1)S(1)} collective-permute-done((bf16[8,16,256]{2,1,0:T(8,128)(2,1)S(1)}, bf16[8,16,256]{2,1,0:T(8,128)(2,1)S(1)}, u32[]{:S(2)}, u32[]{:S(2)}) %collective-permute-start.8) | collective-permute-done | bytes 65568 | tf_op jit(solution)/shard_map/ppermute | solution.py:511
  90.3 1.5 %finish.1 = (bf16[1024,256]{1,0:T(8,128)(2,1)}, bf16[1024,256]{1,0:T(8,128)(2,1)}, bf16[1024,256]{1,0:T(8,128)(2,1)}, bf16[1024,256]{1,0:T(8,128)(2,1)}) custom-call(bf16[8,2,4,32,256]{4,3,2,1,0:T(8,128)(2,1)S(1)} %bitcast.17, bf16[1024,256]{1,0:T(8,128)(2,1)S(1)} %copy-done.1, bf16[1024,256]{1,0:T(8,128)(2,1)S(1)} %copy-done.3, ...), custom_call_target="tpu_custom_call" | custom-call | tf_op jit(solution)/shard_map/finish/pallas_call | solution.py:157
  (56 shorter events, 13.5 us)
Async XLA Ops:
  0.6 1.0 %copy-start = (bf16[1024,256]{1,0:T(8,128)(2,1)S(1)}, bf16[1024,256]{1,0:T(8,128)(2,1)}, u32[]{:S(2)}) copy-start(bf16[1024,256]{1,0:T(8,128)(2,1)} %refs_1_.5) | copy-start | bytes 1572868
  1.7 1.0 %copy-start.2 = (bf16[1024,256]{1,0:T(8,128)(2,1)S(1)}, bf16[1024,256]{1,0:T(8,128)(2,1)}, u32[]{:S(2)}) copy-start(bf16[1024,256]{1,0:T(8,128)(2,1)} %refs_2_.6) | copy-start | bytes 1572868
  2.7 1.0 %copy-start.4 = (bf16[1024,256]{1,0:T(8,128)(2,1)S(1)}, bf16[1024,256]{1,0:T(8,128)(2,1)}, u32[]{:S(2)}) copy-start(bf16[1024,256]{1,0:T(8,128)(2,1)} %refs_3_.5) | copy-start | bytes 1572868
  7.3 6.5 %copy-start.1 = (bf16[1024,256]{1,0:T(8,128)(2,1)S(1)}, bf16[1024,256]{1,0:T(8,128)(2,1)}, u32[]{:S(2)}) copy-start(bf16[1024,256]{1,0:T(8,128)(2,1)} %refs_1_.5) | copy-start | bytes 1572868
  7.3 6.5 %copy-start.3 = (bf16[1024,256]{1,0:T(8,128)(2,1)S(1)}, bf16[1024,256]{1,0:T(8,128)(2,1)}, u32[]{:S(2)}) copy-start(bf16[1024,256]{1,0:T(8,128)(2,1)} %refs_2_.6) | copy-start | bytes 1572868
  7.3 6.5 %copy-start.5 = (bf16[1024,256]{1,0:T(8,128)(2,1)S(1)}, bf16[1024,256]{1,0:T(8,128)(2,1)}, u32[]{:S(2)}) copy-start(bf16[1024,256]{1,0:T(8,128)(2,1)} %refs_3_.5) | copy-start | bytes 1572868
  7.4 6.5 %copy-start.7 = (bf16[1024,256]{1,0:T(8,128)(2,1)S(1)}, bf16[1024,256]{1,0:T(8,128)(2,1)}, u32[]{:S(2)}) copy-start(bf16[1024,256]{1,0:T(8,128)(2,1)} %refs_4_.1) | copy-start | bytes 1572868
  7.4 41.1 %all-to-all-start = ((bf16[16,128,256]{2,1,0:T(8,128)(2,1)}), bf16[16,128,256]{2,1,0:T(8,128)(2,1)}, u32[]{:S(2)}, u32[]{:S(2)}) async-start(bf16[16,128,256]{2,1,0:T(8,128)(2,1)} %bitcast), calls=%async_computation | async-start | bytes 2097152 | tf_op jit(solution)/shard_map/all_to_all | solution.py:478
  13.8 2.6 %copy-start.18 = (f32[16,2048]{1,0:T(8,128)S(1)}, f32[16,2048]{1,0:T(8,128)}, u32[]{:S(2)}) copy-start(f32[16,2048]{1,0:T(8,128)} %param.10) | copy-start | bytes 393220
  16.2 2.4 %collective-permute-start = (bf16[4,128,256]{2,1,0:T(8,128)(2,1)S(1)}, bf16[4,128,256]{2,1,0:T(8,128)(2,1)S(1)}, u32[]{:S(2)}, u32[]{:S(2)}) collective-permute-start(bf16[4,128,256]{2,1,0:T(8,128)(2,1)S(1)} %bitcast.20), channel_id=1, source_target_pairs={{0,1},{1,0},{2,3},{3,2},{4,5},{5,4},{6,7},{7,6},{8,9},{9,8},{10,11... | collective-permute-start | bytes 786440 | tf_op jit(solution)/shard_map/ppermute | solution.py:212
  17.1 17.9 %collective-permute-start.3 = (bf16[8,16,256]{2,1,0:T(8,128)(2,1)}, bf16[8,16,256]{2,1,0:T(8,128)(2,1)}, u32[]{:S(2)}, u32[]{:S(2)}) collective-permute-start(bf16[8,16,256]{2,1,0:T(8,128)(2,1)} %bitcast.16), channel_id=1, source_target_pairs={{0,16},{16,0},{1,17},{17,1},{2,18},{18,2},{3,19},{19,3},{4,20},{20... | collective-permute-start | bytes 196616 | tf_op jit(solution)/shard_map/ppermute | solution.py:483
  19.3 27.0 %copy-start.8 = (bf16[512,1024]{1,0:T(8,128)(2,1)S(1)}, bf16[512,1024]{1,0:T(8,128)(2,1)}, u32[]{:S(2)}) copy-start(bf16[512,1024]{1,0:T(8,128)(2,1)} %constant.12.clone.refs_2_.refs_6_.refs_5_) | copy-start | bytes 3145732
  19.3 13.7 %collective-permute-start.1 = (bf16[4,128,256]{2,1,0:T(8,128)(2,1)}, bf16[4,128,256]{2,1,0:T(8,128)(2,1)}, u32[]{:S(2)}, u32[]{:S(2)}) collective-permute-start(bf16[4,128,256]{2,1,0:T(8,128)(2,1)} %pad_maximum_fusion), channel_id=1, source_target_pairs={{0,2},{1,3},{2,0},{3,1},{4,6},{5,7},{6,4},{7,5},{8,10},{9,11},{10,... | collective-permute-start | bytes 786440 | tf_op jit(solution)/shard_map/ppermute | solution.py:212
  34.9 12.9 %collective-permute-start.2 = (bf16[4,128,256]{2,1,0:T(8,128)(2,1)S(1)}, bf16[4,128,256]{2,1,0:T(8,128)(2,1)S(1)}, u32[]{:S(2)}, u32[]{:S(2)}) collective-permute-start(bf16[4,128,256]{2,1,0:T(8,128)(2,1)S(1)} %pad_maximum_fusion.1), channel_id=1, source_target_pairs={{0,4},{1,5},{2,6},{3,7},{4,0},{5,1},{6,2},{7,3},{8,12},{9,13},{10,... | collective-permute-start | bytes 786440 | tf_op jit(solution)/shard_map/ppermute | solution.py:212
  35.9 5.1 %collective-permute-start.5 = (bf16[16,16,256]{2,1,0:T(8,128)(2,1)S(1)}, bf16[16,16,256]{2,1,0:T(8,128)(2,1)S(1)}, u32[]{:S(2)}, u32[]{:S(2)}) collective-permute-start(bf16[16,16,256]{2,1,0:T(8,128)(2,1)S(1)} %maximum_select_fusion), channel_id=1, source_target_pairs={{0,8},{1,0},{2,9},{3,1},{4,10},{5,2},{6,11},{7,3},{8,12},{9,4},{10... | collective-permute-start | bytes 393224 | tf_op jit(solution)/shard_map/ppermute | solution.py:490
  37.5 8.9 %collective-permute-start.4 = (bf16[16,16,256]{2,1,0:T(8,128)(2,1)S(1)}, bf16[16,16,256]{2,1,0:T(8,128)(2,1)S(1)}, u32[]{:S(2)}, u32[]{:S(2)}) collective-permute-start(bf16[16,16,256]{2,1,0:T(8,128)(2,1)S(1)} %maximum_select_fusion), channel_id=1, source_target_pairs={{0,0},{1,8},{2,1},{3,9},{4,2},{5,10},{6,3},{7,11},{8,4},{9,12},{10... | collective-permute-start | bytes 393224 | tf_op jit(solution)/shard_map/ppermute | solution.py:489
  48.5 1.2 %copy-start.12 = (f32[8,32,1024]{2,1,0:T(8,128)S(1)}, f32[8,32,1024]{2,1,0:T(8,128)}, u32[]{:S(2)}) copy-start(f32[8,32,1024]{2,1,0:T(8,128)} %copy-done.11) | copy-start | bytes 3145732
  50.7 1.2 %copy-start.16 = (bf16[1024,512]{1,0:T(8,128)(2,1)S(1)}, bf16[1024,512]{1,0:T(8,128)(2,1)}, u32[]{:S(2)}) copy-start(bf16[1024,512]{1,0:T(8,128)(2,1)} %constant.13.clone.refs_7_.refs_6_) | copy-start | bytes 3145732
  59.7 30.6 %all-to-all-start.1 = ((bf16[8,2,128,256]{3,2,1,0:T(8,128)(2,1)}), bf16[8,2,128,256]{3,2,1,0:T(8,128)(2,1)S(1)}, u32[]{:S(2)}, u32[]{:S(2)}) async-start(bf16[8,2,128,256]{3,2,1,0:T(8,128)(2,1)} %copy-done.10), calls=%async_computation.1 | async-start | bytes 2097152 | tf_op jit(solution)/shard_map/all_to_all | solution.py:499
  63.2 1.2 %copy-start.9 = (bf16[512,1024]{1,0:T(8,128)(2,1)S(1)}, bf16[512,1024]{1,0:T(8,128)(2,1)}, u32[]{:S(2)}) copy-start(bf16[512,1024]{1,0:T(8,128)(2,1)} %constant.12.clone.refs_2_.refs_6_.refs_5_) | copy-start | bytes 3145732
  65.4 1.2 %copy-start.17 = (bf16[1024,512]{1,0:T(8,128)(2,1)S(1)}, bf16[1024,512]{1,0:T(8,128)(2,1)}, u32[]{:S(2)}) copy-start(bf16[1024,512]{1,0:T(8,128)(2,1)} %constant.13.clone.refs_7_.refs_6_) | copy-start | bytes 3145732
  71.5 7.9 %collective-permute-start.6 = (bf16[8,16,256]{2,1,0:T(8,128)(2,1)S(1)}, bf16[8,16,256]{2,1,0:T(8,128)(2,1)S(1)}, u32[]{:S(2)}, u32[]{:S(2)}) collective-permute-start(bf16[8,16,256]{2,1,0:T(8,128)(2,1)S(1)} %get-tuple-element.20), channel_id=1, source_target_pairs={{0,8},{1,9},{2,10},{3,11},{4,12},{5,13},{6,14},{7,15},{8,0},{9,1},... | collective-permute-start | bytes 196616 | tf_op jit(solution)/shard_map/ppermute | solution.py:504
  79.4 7.2 %collective-permute-start.7 = (bf16[8,16,256]{2,1,0:T(8,128)(2,1)S(1)}, bf16[8,16,256]{2,1,0:T(8,128)(2,1)S(1)}, u32[]{:S(2)}, u32[]{:S(2)}) collective-permute-start(bf16[8,16,256]{2,1,0:T(8,128)(2,1)S(1)} %get-tuple-element.21), channel_id=1, source_target_pairs={{0,0},{1,2},{2,4},{3,6},{4,8},{5,10},{6,12},{7,14},{8,1},{9,3},{10... | collective-permute-start | bytes 196616 | tf_op jit(solution)/shard_map/ppermute | solution.py:510
  81.4 8.3 %collective-permute-start.8 = (bf16[8,16,256]{2,1,0:T(8,128)(2,1)S(1)}, bf16[8,16,256]{2,1,0:T(8,128)(2,1)S(1)}, u32[]{:S(2)}, u32[]{:S(2)}) collective-permute-start(bf16[8,16,256]{2,1,0:T(8,128)(2,1)S(1)} %get-tuple-element.22), channel_id=1, source_target_pairs={{0,16},{1,18},{2,20},{3,22},{4,24},{5,26},{6,28},{7,30},{8,17},{9,... | collective-permute-start | bytes 196616 | tf_op jit(solution)/shard_map/ppermute | solution.py:511
  (6 other events, 5.6 us)
where the time goes:
time: 92.7 us; the launch traced here: 91.8 us
  waiting for transfers between devices  29.9 us (32%)
  starting transfers between devices  23.4 us (25%)
  Pallas kernels  18.4 us (20%)
  local copies, waits for them, and re-layouts  16.6 us (18%)
  other arithmetic  2.63 us (3%)
    unnamed x38, local copies, waits for them, and re-layouts  13.6 us
    ppermute x3, waiting for transfers between devices, swap(): return lax.ppermute(array, 'ctx', [(i, i ^ bit) for i in range(blocks)])  11.6 us
    pallas_call x1, Pallas kernels, convolve(): pl.pallas_call(lambda *refs: convolve_kernel(half_blocks, slots, *refs),...  6.83 us
    all_to_all x1, starting transfers between devices, body(): lax.all_to_all(near.reshape(blocks, repeats * owned, tokens), 'ctx', spli...  6.43 us
    ppermute x1, waiting for transfers between devices, body(): lax.ppermute(give, 'ctx', [(i, (i + half_blocks) % blocks) for i in range...  5.34 us
    ppermute x1, waiting for transfers between devices, body(): lax.ppermute(tap_all, 'ctx', [(i, i // 2 + i % 2 * half_blocks) for i in...  5.28 us
    pallas_call x2, Pallas kernels, gate(): pl.pallas_call(lambda *refs: gate_kernel(near, half_blocks, *refs), in_sp...  4.85 us
    pallas_call x1, Pallas kernels, correlate(): pl.pallas_call(lambda *refs: correlate_kernel(half_blocks, slots, *refs),...  4.81 us
  transfers between devices with their start and end apart: 11, of which 5 were waited for; matrix products, arithmetic and copies ran while one was open for 6% of the time, Pallas kernels for 8%

commit v1 on v0

--- a/solution.py
+++ b/solution.py
@@ -11,7 +11,7 @@
 
 LANES = 128
 SUBLANES = 8
-VMEM_BYTES = 48 * 1024 * 1024
+MEBI = 1024 * 1024
 
 
 def dft_tables(size):
@@ -47,7 +47,7 @@
 def gate_kernel(near, half_blocks, pre_ref, value_ref, post_ref, cot_ref, *refs):
     out_refs, (left_ref, right_ref, result_ref, in_sems, out_sems) = refs[:-5], refs[-5:]
     repeats, rows, tokens = left_ref.shape
-    share = rows // half_blocks
+    share = rows // (2 * half_blocks)
     half, me = place(half_blocks)
     use_gated = half == 0 if near else half != 0
 
@@ -75,76 +75,71 @@
         for copy in fetch(r, pre_ref, value_ref):
             copy.wait()
         product = left_ref[r].astype(jnp.float32) * right_ref[r].astype(jnp.float32)
-        product = product.astype(jnp.bfloat16).reshape(half_blocks, share, tokens)
+        product = product.astype(jnp.bfloat16).reshape(2, half_blocks, share, tokens)
+        for side in range(2):
+            if near:
+                result_ref[r, :, side] = product[side]
+            else:
+                result_ref[:, r, side] = product[side]
         if near:
-            result_ref[r] = product
-            for side in range(2):
-                copy = pltpu.make_async_copy(result_ref.at[r], out_refs[0].at[side, :, r], out_sems.at[side, r])
+            for copy_at in range(2):
+                copy = pltpu.make_async_copy(result_ref.at[r], out_refs[0].at[copy_at, :, r], out_sems.at[copy_at, r])
                 copy.start()
                 pending.append(copy)
-        else:
-            result_ref[:, r] = product
     if not near:
-        even_ref, odd_ref = out_refs
-        for at in range(half_blocks // 2):
-            slot = slot_order(half_blocks)[at]
-            for side, target in ((0, even_ref), (1, odd_ref)):
-                source = result_ref.at[jnp.bitwise_xor(me, slot + side)]
-                copy = pltpu.make_async_copy(source, target.at[at], out_sems.at[side, at])
-                copy.start()
-                pending.append(copy)
+        for slot in range(half_blocks):
+            source = result_ref.at[jnp.bitwise_xor(me, slot)]
+            copy = pltpu.make_async_copy(source, out_refs[slot], out_sems.at[slot])
+            copy.start()
+            pending.append(copy)
     for copy in pending:
         copy.wait()
-
-
-def slot_order(half_blocks):
-    return [s for s in range(0, half_blocks, 2) if not s & 2] + [s for s in range(0, half_blocks, 2) if s & 2]
 
 
 def gate(near, arrays, repeats, half_blocks):
     rows_all, tokens = arrays[0].shape
     rows = rows_all // repeats
-    share = rows // half_blocks
+    share = rows // (2 * half_blocks)
     if near:
-        shapes = [(2, half_blocks, repeats, share, tokens)]
-        held, count = (repeats, half_blocks, share, tokens), repeats
+        shapes = [(2, half_blocks, repeats, 2, share, tokens)]
+        held, sems = (repeats, half_blocks, 2, share, tokens), (2, repeats)
     else:
-        shapes = [(half_blocks // 2, repeats, share, tokens)] * 2
-        held, count = (half_blocks, repeats, share, tokens), half_blocks // 2
-    result = pl.pallas_call(
+        shapes = [(repeats, 2, share, tokens)] * half_blocks
+        held, sems = (half_blocks, repeats, 2, share, tokens), (half_blocks,)
+    return pl.pallas_call(
         lambda *refs: gate_kernel(near, half_blocks, *refs),
-        in_specs=[pl.BlockSpec(memory_space=pl.ANY)] * 4,
-        out_specs=[pl.BlockSpec(memory_space=pl.ANY)] * len(shapes),
+        in_specs=[pl.BlockSpec(memory_space=pltpu.HBM)] * 4,
+        out_specs=[pl.BlockSpec(memory_space=pltpu.HBM)] * len(shapes),
         out_shape=[jax.ShapeDtypeStruct(shape, jnp.bfloat16) for shape in shapes],
         scratch_shapes=[
             pltpu.VMEM((repeats, rows, tokens), jnp.bfloat16),
             pltpu.VMEM((repeats, rows, tokens), jnp.bfloat16),
             pltpu.VMEM(held, jnp.bfloat16),
             pltpu.SemaphoreType.DMA((2, repeats)),
-            pltpu.SemaphoreType.DMA((2, count)),
+            pltpu.SemaphoreType.DMA(sems),
         ],
-        compiler_params=pltpu.CompilerParams(vmem_limit_bytes=VMEM_BYTES),
+        compiler_params=pltpu.CompilerParams(vmem_limit_bytes=6 * MEBI),
         cost_estimate=pl.CostEstimate(flops=rows_all * tokens, bytes_accessed=8 * rows_all * tokens, transcendentals=0),
         name="gate_near" if near else "gate_own",
     )(*arrays)
-    return result[0] if near else result
 
 
 def finish_kernel(half_blocks, recv_ref, pre_ref, value_ref, post_ref, cot_ref, *refs):
     out_refs, (held_ref, sems) = refs[:4], refs[4:]
-    repeats = recv_ref.shape[2]
+    repeats, sides = recv_ref.shape[2:4]
     rows, tokens = held_ref.shape[2:]
     half, _ = place(half_blocks)
     pending = []
-    for r in range(repeats):
-        at = pl.ds(r * rows, rows)
-        conv = recv_ref[:, half, r].reshape(rows, tokens).astype(jnp.float32)
-        grad = recv_ref[:, 1 - half, r].reshape(rows, tokens).astype(jnp.float32)
+    for part in range(repeats * sides):
+        r, side = part // sides, part % sides
+        at = pl.ds(part * rows, rows)
+        conv = recv_ref[:, half, r, side].reshape(rows, tokens).astype(jnp.float32)
+        grad = recv_ref[:, 1 - half, r, side].reshape(rows, tokens).astype(jnp.float32)
         for which, (factor_ref, result) in enumerate(
             ((post_ref, conv), (value_ref, grad), (pre_ref, grad), (cot_ref, conv))
         ):
-            held_ref[which, r] = (factor_ref[at].astype(jnp.float32) * result).astype(jnp.bfloat16)
-            copy = pltpu.make_async_copy(held_ref.at[which, r], out_refs[which].at[at], sems.at[which, r])
+            held_ref[which, part] = (factor_ref[at].astype(jnp.float32) * result).astype(jnp.bfloat16)
+            copy = pltpu.make_async_copy(held_ref.at[which, part], out_refs[which].at[at], sems.at[which, part])
             copy.start()
             pending.append(copy)
     for copy in pending:
@@ -152,40 +147,41 @@
 
 
 def finish(received, pre_gate, values, post_gate, cotangent):
-    half_blocks, _, repeats, share, tokens = received.shape
-    rows = half_blocks * share
+    half_blocks, _, repeats, sides, share, tokens = received.shape
+    parts, rows = repeats * sides, half_blocks * share
     return pl.pallas_call(
         lambda *refs: finish_kernel(half_blocks, *refs),
         in_specs=[pl.BlockSpec(memory_space=pltpu.VMEM)] * 5,
-        out_specs=[pl.BlockSpec(memory_space=pl.ANY)] * 4,
+        out_specs=[pl.BlockSpec(memory_space=pltpu.HBM)] * 4,
         out_shape=[jax.ShapeDtypeStruct(pre_gate.shape, jnp.bfloat16)] * 4,
         scratch_shapes=[
-            pltpu.VMEM((4, repeats, rows, tokens), jnp.bfloat16),
-            pltpu.SemaphoreType.DMA((4, repeats)),
+            pltpu.VMEM((4, parts, rows, tokens), jnp.bfloat16),
+            pltpu.SemaphoreType.DMA((4, parts)),
         ],
-        compiler_params=pltpu.CompilerParams(vmem_limit_bytes=VMEM_BYTES),
+        compiler_params=pltpu.CompilerParams(vmem_limit_bytes=8 * MEBI),
         name="finish",
     )(received, pre_gate, values, post_gate, cotangent)
 
 
-def taps_kernel(half_blocks, first_ref, second_ref, forward_ref, out_ref, stage_ref):
+def taps_kernel(half_blocks, groups, *refs):
+    piece_refs, (forward_ref, out_ref, stage_ref) = refs[:-3], refs[-3:]
     count, rows, width = out_ref.shape
     size = width // 2
-    share, tokens = first_ref.shape[1:]
-    merge = size // tokens
+    share, lags = piece_refs[0].shape
     half, _ = place(half_blocks)
-    low, high = first_ref[...], second_ref[...]
-    ordered = (jnp.where(half == 0, low, high), jnp.where(half == 0, high, low))
-    for part in range(2):
-        for k in range(count):
-            for q in range(merge):
-                stage_ref[k, pl.ds(part * share, share), pl.ds(q * tokens, tokens)] = ordered[part][k * merge + q]
+    group = lax.axis_index("dp")
+    for at, ref in enumerate(piece_refs):
+        side = half if at < 2 else 1 - half
+        first = (group if at % 2 == 0 else 1 - group) * (lags // size)
+        for k in range(lags // size):
+            stage_ref[first + k, pl.ds(pl.multiple_of(side * share, share), share)] = ref[:, k * size : (k + 1) * size]
     spectrum = dot(stage_ref[...].reshape(count * rows, size), forward_ref[...]).reshape(count, rows, width)
     turn = jnp.where(half == 0, 1.0, -1.0).astype(jnp.float32)
     sign = alternating()[:1]
     for k in range(count):
         for strip in range(size // LANES):
-            re, im = slice(2 * strip * LANES, (2 * strip + 1) * LANES), slice((2 * strip + 1) * LANES, (2 * strip + 2) * LANES)
+            re = slice(2 * strip * LANES, (2 * strip + 1) * LANES)
+            im = slice((2 * strip + 1) * LANES, (2 * strip + 2) * LANES)
             real, imag = spectrum[k, :, re], spectrum[k, :, im]
             if k > 0:
                 real, imag = real - sign * spectrum[k - 1, :, im], imag + sign * spectrum[k - 1, :, re]
@@ -193,47 +189,17 @@
             out_ref[k, :, im] = turn * imag
 
 
-def transform_taps(first, second, half_blocks, size, forward):
-    blocks, share, tokens = first.shape
-    count = blocks * tokens // size
+def transform_taps(pieces, half_blocks, groups, forward):
+    share, lags = pieces[0].shape
+    size = forward.shape[0]
+    count = groups * lags // size
     return pl.pallas_call(
-        lambda *refs: taps_kernel(half_blocks, *refs),
+        lambda *refs: taps_kernel(half_blocks, groups, *refs),
         out_shape=jax.ShapeDtypeStruct((count, 2 * share, 2 * size), jnp.float32),
         scratch_shapes=[pltpu.VMEM((count, 2 * share, size), jnp.bfloat16)],
-        compiler_params=pltpu.CompilerParams(vmem_limit_bytes=VMEM_BYTES),
+        compiler_params=pltpu.CompilerParams(vmem_limit_bytes=8 * MEBI),
         name="taps",
-    )(first, second, forward)
-
-
-def exchange_own(even, odd, half_blocks):
-    blocks = 2 * half_blocks
-
-    def swap(array, bit):
-        return lax.ppermute(array, "ctx", [(i, i ^ bit) for i in range(blocks)])
-
-    order = slot_order(half_blocks)
-    groups = [(list(order), even), ([s + 1 for s in order], swap(odd, 1))]
-    bit = 2
-    while bit < half_blocks:
-        kept, leaving, leaving_slots = [], [], []
-        for slots, array in groups:
-            stays = [at for at, s in enumerate(slots) if not s & bit]
-            goes = [at for at, s in enumerate(slots) if s & bit]
-            kept.append(([slots[at] for at in stays], take(array, stays)))
-            if goes:
-                leaving.append(take(array, goes))
-                leaving_slots += [slots[at] for at in goes]
-        groups = [g for g in kept if g[0]] + [(leaving_slots, swap(jnp.concatenate(leaving), bit))]
-        bit *= 2
-    return groups
-
-
-def take(array, rows):
-    if not rows:
-        return None
-    if rows == list(range(rows[0], rows[0] + len(rows))):
-        return array[rows[0] : rows[0] + len(rows)]
-    return jnp.concatenate([array[at : at + 1] for at in rows])
+    )(*pieces, forward)
 
 
 def add(total, term):
@@ -248,17 +214,26 @@
     return a[0] * b[0] + a[1] * b[1], a[0] * b[1] - a[1] * b[0]
 
 
-def convolve_kernel(half_blocks, slots, near_ref, *refs):
-    own_refs = refs[: len(slots)]
-    filt_ref, forward_ref, inverse_ref, out_ref, stage_ref, spec_ref, prod_ref = refs[len(slots) :]
+def transform(stage_ref, forward_ref, spec_ref):
+    width = spec_ref.shape[-1]
+    staged = stage_ref[...].reshape(-1, stage_ref.shape[-1])
+    for strip in range(width // (2 * LANES)):
+        columns = slice(2 * strip * LANES, 2 * (strip + 1) * LANES)
+        result = dot(staged, forward_ref[:, columns])
+        spec_ref[:, :, :, columns] = result.reshape(spec_ref.shape[:-1] + (2 * LANES,))
+
+
+def convolve_kernel(half_blocks, near_ref, *refs):
+    own_refs = refs[:half_blocks]
+    filt_ref, forward_ref, inverse_ref, out_ref, stage_ref, spec_ref, prod_ref, held_ref, sems = refs[half_blocks:]
     _, count, rows, width = spec_ref.shape
     size = width // 2
     tokens = near_ref.shape[2]
     merge = size // tokens
     filters = filt_ref.shape[1]
     half, _ = place(half_blocks)
-    fill_stage(half_blocks, merge, near_ref, own_refs, slots, stage_ref)
-    spec_ref[...] = dot(stage_ref[...].reshape(3 * count * rows, size), forward_ref[...]).reshape(spec_ref.shape)
+    fill_stage(half_blocks, merge, near_ref, own_refs, stage_ref)
+    transform(stage_ref, forward_ref, spec_ref)
 
     @pl.loop(0, rows // SUBLANES)
     def _(tile):
@@ -287,19 +262,25 @@
                     total = add(total, conj_times(taps[count + out - k], far[k]))
                 prod_ref[1, out, row, real_of(strip)], prod_ref[1, out, row, imag_of(strip)] = total
 
-    result = dot(prod_ref[...].astype(jnp.bfloat16).reshape(2 * count * rows, width), inverse_ref[...])
-    result = result.astype(jnp.bfloat16).reshape(2, count, rows, size)
-    for k in range(count):
-        flipped = count - 1 - k
-        outer = jnp.where(half == 0, k, flipped)
-        inner = jnp.where(half == 0, flipped, k)
-        for q in range(merge):
-            lanes = slice(q * tokens, (q + 1) * tokens)
-            out_ref[outer * merge + q, 0] = result[0, k, :, lanes]
-            out_ref[inner * merge + q, 1] = result[1, k, :, lanes]
-
-
-def fill_stage(half_blocks, merge, near_ref, own_refs, slots, stage_ref):
+    pending = []
+    for which in range(2):
+        result = dot(prod_ref[which].astype(jnp.bfloat16).reshape(count * rows, width), inverse_ref[...])
+        result = result.astype(jnp.bfloat16).reshape(count, rows, size)
+        for k in range(count):
+            flipped = count - 1 - k
+            block = jnp.where(half == which, k, flipped)
+            for q in range(merge):
+                held_ref[which, k, q] = result[k, :, q * tokens : (q + 1) * tokens]
+                copy = pltpu.make_async_copy(
+                    held_ref.at[which, k, q], out_ref.at[block * merge + q, which], sems.at[which, k, q]
+                )
+                copy.start()
+                pending.append(copy)
+    for copy in pending:
+        copy.wait()
+
+
+def fill_stage(half_blocks, merge, near_ref, own_refs, stage_ref):
     count = half_blocks // merge
     tokens = near_ref.shape[2]
     half, me = place(half_blocks)
@@ -311,43 +292,46 @@
             lanes = pl.ds(q * tokens, tokens)
             stage_ref[0, k, :, lanes] = near_ref[half * half_blocks + outer * merge + q]
             stage_ref[2, k, :, lanes] = near_ref[(1 - half) * half_blocks + inner * merge + q]
-    for group, ref in zip(slots, own_refs):
-        for at, slot in enumerate(group):
-            position = jnp.bitwise_xor(me, slot)
-            block = position // merge
-            k = jnp.where(half == 0, count - 1 - block, block)
-            start = pl.multiple_of(lax.rem(position, merge) * tokens, tokens)
-            stage_ref[1, k, :, pl.ds(start, tokens)] = ref[at]
+    for slot, ref in enumerate(own_refs):
+        position = jnp.bitwise_xor(me, slot)
+        block = position // merge
+        k = jnp.where(half == 0, count - 1 - block, block)
+        start = pl.multiple_of(lax.rem(position, merge) * tokens, tokens)
+        stage_ref[1, k, :, pl.ds(start, tokens)] = ref[...]
 
 
 def convolve(near, own, filt, half_blocks, tables):
     forward, inverse = tables
     _, rows, tokens = near.shape
     size = forward.shape[0]
-    count = half_blocks * tokens // size
-    slots = [group for group, _ in own]
+    merge = size // tokens
+    count = half_blocks // merge
     pairs = count * (2 * count + 1)
     return pl.pallas_call(
-        lambda *refs: convolve_kernel(half_blocks, slots, *refs),
+        lambda *refs: convolve_kernel(half_blocks, *refs),
+        out_specs=pl.BlockSpec(memory_space=pltpu.HBM),
         out_shape=jax.ShapeDtypeStruct((half_blocks, 2, rows, tokens), jnp.bfloat16),
         scratch_shapes=[
             pltpu.VMEM((3, count, rows, size), jnp.bfloat16),
             pltpu.VMEM((3, count, rows, 2 * size), jnp.float32),
             pltpu.VMEM((2, count, rows, 2 * size), jnp.float32),
+            pltpu.VMEM((2, count, merge, rows, tokens), jnp.bfloat16),
+            pltpu.SemaphoreType.DMA((2, count, merge)),
         ],
-        compiler_params=pltpu.CompilerParams(vmem_limit_bytes=VMEM_BYTES),
+        compiler_params=pltpu.CompilerParams(vmem_limit_bytes=28 * MEBI),
         cost_estimate=pl.CostEstimate(
             flops=20 * count * rows * size * size + 8 * pairs * rows * size,
             bytes_accessed=10 * count * rows * size,
             transcendentals=0,
         ),
         name="convolve",
-    )(near, *[array for _, array in own], filt, forward, inverse)
-
-
-def correlate_kernel(half_blocks, slots, near_ref, *refs):
-    own_refs = refs[: len(slots)]
-    forward_ref, inverse_ref, keep_ref, give_ref, stage_ref, spec_ref, local_ref, cross_ref, joint_ref = refs[len(slots) :]
+    )(near, *own, filt, forward, inverse)
+
+
+def correlate_kernel(half_blocks, near_ref, *refs):
+    own_refs = refs[:half_blocks]
+    forward_ref, inverse_ref, mine_ref, theirs_ref, give_ref = refs[half_blocks : half_blocks + 5]
+    stage_ref, spec_ref, local_ref, cross_ref, joint_ref, held_ref = refs[half_blocks + 5 :]
     _, count, rows, width = spec_ref.shape
     size = width // 2
     tokens = near_ref.shape[2]
@@ -357,8 +341,8 @@
     kept = filters // 2
     half, _ = place(half_blocks)
     turn = jnp.where(half == 0, 1.0, -1.0).astype(jnp.float32)
-    fill_stage(half_blocks, merge, near_ref, own_refs, slots, stage_ref)
-    spec_ref[...] = dot(stage_ref[...].reshape(3 * count * rows, size), forward_ref[...]).reshape(spec_ref.shape)
+    fill_stage(half_blocks, merge, near_ref, own_refs, stage_ref)
+    transform(stage_ref, forward_ref, spec_ref)
 
     def products(other, row_at, strip, lags):
         totals = [None] * len(lags)
@@ -420,13 +404,13 @@
     join(cross_ref, pl.ds(0, kept), 2 * count, 0)
     join(local_ref, other, count, 2 * count)
     result = dot(joint_ref[...].reshape(3 * count * kept, width), inverse_ref[...]).reshape(3 * count, kept, size)
-    for k in range(3 * count):
-        for q in range(merge):
-            piece = result[k, :, q * tokens : (q + 1) * tokens]
-            if k < 2 * count:
-                keep_ref[k * merge + q] = piece
-            else:
-                give_ref[(k - 2 * count) * merge + q] = piece.astype(jnp.bfloat16)
+    held_ref[...] = result[: 2 * count].reshape(2, count, kept, size)
+    group = lax.axis_index("dp")
+    for k in range(count):
+        columns = slice(k * size, (k + 1) * size)
+        mine_ref[:, columns] = held_ref[group, k]
+        theirs_ref[:, columns] = held_ref[1 - group, k].astype(jnp.bfloat16)
+        give_ref[:, columns] = result[2 * count + k].astype(jnp.bfloat16)
 
 
 def correlate(near, own, filters, half_blocks, tables):
@@ -434,14 +418,14 @@
     _, rows, tokens = near.shape
     size = forward.shape[0]
     count = half_blocks * tokens // size
-    slots = [group for group, _ in own]
     pairs = count * (2 * count + 1)
     kept = filters // 2
     return pl.pallas_call(
-        lambda *refs: correlate_kernel(half_blocks, slots, *refs),
+        lambda *refs: correlate_kernel(half_blocks, *refs),
         out_shape=[
-            jax.ShapeDtypeStruct((2 * half_blocks, kept, tokens), jnp.float32),
-            jax.ShapeDtypeStruct((half_blocks, kept, tokens), jnp.bfloat16),
+            jax.ShapeDtypeStruct((kept, count * size), jnp.float32),
+            jax.ShapeDtypeStruct((kept, count * size), jnp.bfloat16),
+            jax.ShapeDtypeStruct((kept, count * size), jnp.bfloat16),
         ],
         scratch_shapes=[
             pltpu.VMEM((3, count, rows, size), jnp.bfloat16),
@@ -449,15 +433,16 @@
             pltpu.VMEM((count, filters, 2 * size), jnp.float32),
             pltpu.VMEM((2 * count, kept, 2 * size), jnp.float32),
             pltpu.VMEM((3 * count, kept, 2 * size), jnp.bfloat16),
+            pltpu.VMEM((2, count, kept, size), jnp.float32),
         ],
-        compiler_params=pltpu.CompilerParams(vmem_limit_bytes=VMEM_BYTES),
+        compiler_params=pltpu.CompilerParams(vmem_limit_bytes=28 * MEBI),
         cost_estimate=pl.CostEstimate(
             flops=14 * count * rows * size * size + 4 * pairs * rows * size,
             bytes_accessed=8 * count * rows * size,
             transcendentals=0,
         ),
         name="correlate",
-    )(near, *[array for _, array in own], forward, inverse)
+    )(near, *own, forward, inverse)
 
 
 def body(pre_gate, values, post_gate, filters, cotangent):
@@ -468,31 +453,30 @@
     local_filters = filters.shape[0]
     repeats = local_rows // (local_filters * blocks)
     owned = 2 * local_filters
-    lags = blocks // groups
     tables = dft_tables(2 * tokens)
-    group = lax.axis_index("dp")
-    half = lax.axis_index("ctx") // half_blocks
     arrays = (pre_gate, values, post_gate, cotangent)
 
-    near = gate(True, arrays, repeats, half_blocks)
+    def swap(array, bit):
+        return array if bit == 0 else lax.ppermute(array, "ctx", [(i, i ^ bit) for i in range(blocks)])
+
+    (near,) = gate(True, arrays, repeats, half_blocks)
     near = lax.all_to_all(
         near.reshape(blocks, repeats * owned, tokens), "ctx", split_axis=0, concat_axis=0, tiled=True
     )
 
-    tap_local = jnp.transpose(filters.reshape(local_filters, lags, tokens), (1, 0, 2)).astype(jnp.bfloat16)
-    tap_other = lax.ppermute(tap_local, "dp", [(0, 1), (1, 0)])
-    tap_all = jnp.where(
-        group == 0,
-        jnp.concatenate([tap_local, tap_other]),
-        jnp.concatenate([tap_other, tap_local]),
-    )
-    first = lax.ppermute(tap_all, "ctx", [(i, i // 2 + (i % 2) * half_blocks) for i in range(blocks)])
-    second = lax.ppermute(tap_all, "ctx", [(i, i // 2 + (1 - i % 2) * half_blocks) for i in range(blocks)])
-    filt = transform_taps(first, second, half_blocks, 2 * tokens, tables[0])
-
-    even, odd = gate(False, arrays, repeats, half_blocks)
-    shape = (half_blocks // 2, repeats * owned, tokens)
-    own = exchange_own(even.reshape(shape), odd.reshape(shape), half_blocks)
+    taps = filters.astype(jnp.bfloat16)
+    across = [(i, blocks + (i ^ half_blocks)) for i in range(blocks)]
+    across = across + [(b, a) for a, b in across]
+    pieces = (
+        taps,
+        lax.ppermute(taps, "dp", [(0, 1), (1, 0)]),
+        swap(taps, half_blocks),
+        lax.ppermute(taps, ("dp", "ctx"), across),
+    )
+    filt = transform_taps(pieces, half_blocks, groups, tables[0])
+
+    own = gate(False, arrays, repeats, half_blocks)
+    own = [swap(piece.reshape(repeats * owned, tokens), slot) for slot, piece in enumerate(own)]
 
     result = convolve(near, own, filt, half_blocks, tables)
     sides = [list(range(half_blocks)), list(range(half_blocks, blocks))]
@@ -500,21 +484,17 @@
         result, "ctx", split_axis=0, concat_axis=0, tiled=True, axis_index_groups=sides
     )
 
-    keep, give = correlate(near, own, owned, half_blocks, tables)
-    taken = lax.ppermute(give, "ctx", [(i, (i + half_blocks) % blocks) for i in range(blocks)])
-    low = keep[:half_blocks] + taken.astype(jnp.float32)
-    high = keep[half_blocks:]
-    mine = jnp.where(group == 0, low, high).astype(jnp.bfloat16)
-    theirs = jnp.where(group == 0, high, low).astype(jnp.bfloat16)
-    home = [(i, 2 * (i % half_blocks) + i // half_blocks) for i in range(blocks)]
-    mine = lax.ppermute(mine, "ctx", home)
-    theirs = lax.ppermute(
-        theirs, ("dp", "ctx"), [(g * blocks + i, (1 - g) * blocks + j) for g in range(groups) for i, j in home]
-    )
-    summed = mine.astype(jnp.float32) + theirs.astype(jnp.float32)
-    filter_grad = jnp.transpose(summed, (1, 0, 2)).reshape(local_filters, lags * tokens)
-
-    returned = returned.reshape(half_blocks, 2, repeats, owned, tokens)
+    mine, theirs, give = correlate(near, own, owned, half_blocks, tables)
+    terms = (
+        lax.ppermute(theirs, "dp", [(0, 1), (1, 0)]),
+        lax.ppermute(give, ("dp", "ctx"), [(i, i ^ half_blocks) for i in range(blocks)]),
+        lax.ppermute(give, ("dp", "ctx"), [(blocks + i, i ^ half_blocks) for i in range(blocks)]),
+    )
+    filter_grad = mine
+    for term in terms:
+        filter_grad = filter_grad + term.astype(jnp.float32)
+
+    returned = returned.reshape(half_blocks, 2, repeats, 2, local_filters, tokens)
     mixed, pre_grad, value_grad, post_grad = finish(returned, pre_gate, values, post_gate, cotangent)
     return (mixed, pre_grad, value_grad, post_grad, filter_grad)
 

time: 92.7 us -> 96.9 us (1.045)
  the two profiles are of different devices: /device:TPU:8 before, /device:TPU:0 now
where the time goes in v1:
time: 96.9 us; the launch traced here: 96 us
  waiting for transfers between devices  31.9 us (33%)
  starting transfers between devices  26.7 us (28%)
  Pallas kernels  20.3 us (21%)
  local copies, waits for them, and re-layouts  15.6 us (16%)
    ppermute x1, waiting for transfers between devices, body(): lax.ppermute(taps, ('dp', 'ctx'), across)  23.2 us
    unnamed x44, local copies, waits for them, and re-layouts  15.6 us
    pallas_call x1, Pallas kernels, convolve(): pl.pallas_call(lambda *refs: convolve_kernel(half_blocks, *refs), out_spe...  8.61 us
    all_to_all x1, starting transfers between devices, body(): lax.all_to_all(near.reshape(blocks, repeats * owned, tokens), 'ctx', spli...  7.57 us
    ppermute x8, starting transfers between devices, swap(): lax.ppermute(array, 'ctx', [(i, i ^ bit) for i in range(blocks)])  6.8 us
    ppermute x1, waiting for transfers between devices, body(): lax.ppermute(give, ('dp', 'ctx'), [(blocks + i, i ^ half_blocks) for i in...  5.36 us
    pallas_call x1, Pallas kernels, correlate(): pl.pallas_call(lambda *refs: correlate_kernel(half_blocks, *refs), out_sh...  4.84 us
    pallas_call x2, Pallas kernels, gate(): pl.pallas_call(lambda *refs: gate_kernel(near, half_blocks, *refs), in_sp...  4.83 us
  transfers between devices with their start and end apart: 15, of which 5 were waited for; matrix products, arithmetic and copies ran while one was open for 1% of the time, Pallas kernels for 8%

profile of v1, /device:TPU:0, one launch (start us, length us, event | category | flops | bytes accessed | tf_op | source)
XLA Modules:
  0.0 96.0 jit_solution(6976436206079303546)
XLA Ops:
  0.6 1.0 %copy-done = bf16[1024,256]{1,0:T(8,128)(2,1)S(1)} copy-done((bf16[1024,256]{1,0:T(8,128)(2,1)S(1)}, bf16[1024,256]{1,0:T(8,128)(2,1)}, u32[]{:S(2)}) %copy-start) | copy-done | bytes 524312
  1.7 1.0 %copy-done.2 = bf16[1024,256]{1,0:T(8,128)(2,1)S(1)} copy-done((bf16[1024,256]{1,0:T(8,128)(2,1)S(1)}, bf16[1024,256]{1,0:T(8,128)(2,1)}, u32[]{:S(2)}) %copy-start.2) | copy-done | bytes 524312
  2.7 1.0 %copy-done.4 = bf16[1024,256]{1,0:T(8,128)(2,1)S(1)} copy-done((bf16[1024,256]{1,0:T(8,128)(2,1)S(1)}, bf16[1024,256]{1,0:T(8,128)(2,1)}, u32[]{:S(2)}) %copy-start.4) | copy-done | bytes 524312
  3.8 1.0 %copy-done.6 = bf16[1024,256]{1,0:T(8,128)(2,1)S(1)} copy-done((bf16[1024,256]{1,0:T(8,128)(2,1)S(1)}, bf16[1024,256]{1,0:T(8,128)(2,1)}, u32[]{:S(2)}) %copy-start.6) | copy-done | bytes 524312
  4.8 2.5 %gate_near.1 = bf16[2,8,4,2,16,256]{5,4,3,2,1,0:T(8,128)(2,1)} custom-call(bf16[1024,256]{1,0:T(8,128)(2,1)S(1)} %copy-done, bf16[1024,256]{1,0:T(8,128)(2,1)S(1)} %copy-done.2, bf16[1024,256]{1,0:T(8,128)(2,1)S(1)} %copy-done.4, bf16[1024,256]{1,0:T(8,128)(2,1)S(1)} %copy-done.6), custom_call_target="tpu_custom_call" | custom-call | flops 262144 | bytes 2097152 | tf_op jit(solution)/shard_map/gate_near/pallas_call | solution.py:109
  7.3 7.6 %all-to-all-start = ((bf16[16,128,256]{2,1,0:T(8,128)(2,1)}), bf16[16,128,256]{2,1,0:T(8,128)(2,1)}, u32[]{:S(2)}, u32[]{:S(2)}) async-start(bf16[16,128,256]{2,1,0:T(8,128)(2,1)} %bitcast), calls=%async_computation | async-start | bytes 2097152 | tf_op jit(solution)/shard_map/all_to_all | solution.py:463
  15.0 3.8 %collective-permute-start.9 = (bf16[16,2048]{1,0:T(8,128)(2,1)S(1)}, bf16[16,2048]{1,0:T(8,128)(2,1)S(1)}, u32[]{:S(2)}, u32[]{:S(2)}) collective-permute-start(bf16[16,2048]{1,0:T(8,128)(2,1)S(1)} %convert_element_type.12.refs_0_), channel_id=1, source_target_pairs={{0,24},{1,25},{2,26},{3,27},{4,28},{5,29},{6,30},{7,31},{8,16},{9,... | collective-permute-start | bytes 196616 | tf_op jit(solution)/shard_map/ppermute | solution.py:474
  19.4 2.3 %gate_own.1 = (bf16[4,2,16,256]{3,2,1,0:T(8,128)(2,1)S(1)}, bf16[4,2,16,256]{3,2,1,0:T(8,128)(2,1)S(1)}, bf16[4,2,16,256]{3,2,1,0:T(8,128)(2,1)S(1)}, bf16[4,2,1...) custom-call(bf16[1024,256]{1,0:T(8,128)(2,1)S(1)} %copy-done.1, ...), custom_call_target="tpu_custom_call" | custom-call | flops 262144 | bytes 2097152 | tf_op jit(solution)/shard_map/gate_own/pallas_call | solution.py:109
  21.9 1.9 %collective-permute-start.1 = (bf16[128,256]{1,0:T(8,128)(2,1)S(1)}, bf16[128,256]{1,0:T(8,128)(2,1)S(1)}, u32[]{:S(2)}, u32[]{:S(2)}) collective-permute-start(bf16[128,256]{1,0:T(8,128)(2,1)S(1)} %bitcast.18), channel_id=1, source_target_pairs={{0,2},{1,3},{2,0},{3,1},{4,6},{5,7},{6,4},{7,5},{8,10},{9,11},{10,... | collective-permute-start | bytes 196616 | tf_op jit(solution)/shard_map/ppermute | solution.py:460
  23.8 23.2 %collective-permute-done.9.refs_3_ = bf16[16,2048]{1,0:T(8,128)(2,1)S(1)} collective-permute-done((bf16[16,2048]{1,0:T(8,128)(2,1)S(1)}, bf16[16,2048]{1,0:T(8,128)(2,1)S(1)}, u32[]{:S(2)}, u32[]{:S(2)}) %collective-permute-start.9) | collective-permute-done | bytes 65568 | tf_op jit(solution)/shard_map/ppermute | solution.py:474
  47.3 2.7 %collective-permute-start.4 = (bf16[128,256]{1,0:T(8,128)(2,1)S(1)}, bf16[128,256]{1,0:T(8,128)(2,1)S(1)}, u32[]{:S(2)}, u32[]{:S(2)}) collective-permute-start(bf16[128,256]{1,0:T(8,128)(2,1)S(1)} %bitcast.15), channel_id=1, source_target_pairs={{0,5},{1,4},{2,7},{3,6},{4,1},{5,0},{6,3},{7,2},{8,13},{9,12},{10,... | collective-permute-start | bytes 196616 | tf_op jit(solution)/shard_map/ppermute | solution.py:460
  50.3 1.4 %collective-permute-start.6 = (bf16[128,256]{1,0:T(8,128)(2,1)S(1)}, bf16[128,256]{1,0:T(8,128)(2,1)S(1)}, u32[]{:S(2)}, u32[]{:S(2)}) collective-permute-start(bf16[128,256]{1,0:T(8,128)(2,1)S(1)} %bitcast.13), channel_id=1, source_target_pairs={{0,7},{1,6},{2,5},{3,4},{4,3},{5,2},{6,1},{7,0},{8,15},{9,14},{10,... | collective-permute-start | bytes 196616 | tf_op jit(solution)/shard_map/ppermute | solution.py:460
  53.7 2.2 %collective-permute-done.5.refs_7_ = bf16[128,256]{1,0:T(8,128)(2,1)S(1)} collective-permute-done((bf16[128,256]{1,0:T(8,128)(2,1)S(1)}, bf16[128,256]{1,0:T(8,128)(2,1)S(1)}, u32[]{:S(2)}, u32[]{:S(2)}) %collective-permute-start.5) | collective-permute-done | bytes 65568 | tf_op jit(solution)/shard_map/ppermute | solution.py:460
  57.2 1.2 %copy-done.12 = f32[8,32,1024]{2,1,0:T(8,128)S(1)} copy-done((f32[8,32,1024]{2,1,0:T(8,128)S(1)}, f32[8,32,1024]{2,1,0:T(8,128)}, u32[]{:S(2)}) %copy-start.12) | copy-done | bytes 1048600
  60.1 1.2 %copy-done.19 = bf16[1024,512]{1,0:T(8,128)(2,1)S(1)} copy-done((bf16[1024,512]{1,0:T(8,128)(2,1)S(1)}, bf16[1024,512]{1,0:T(8,128)(2,1)}, u32[]{:S(2)}) %copy-start.19) | copy-done | bytes 1048600
  61.3 8.6 %convolve.1 = bf16[8,2,128,256]{3,2,1,0:T(8,128)(2,1)S(1)} custom-call(bf16[16,128,256]{2,1,0:T(8,128)(2,1)} %all-to-all-done.refs_0_, bf16[128,256]{1,0:T(8,128)(2,1)S(1)} %bitcast.11, bf16[128,256]{1,0:T(8,128)(2,1)S(1)} %collective-permute-done.refs_2_, bf16[128,256]{1,0:T(8,128)(2,1)S(1)} %collective-permute-done.1.refs_3_, ...), custom_call_target="tpu_custom_call" | custom-call | flops 2703228928 | bytes 2621440 | tf_op jit(solution)/shard_map/convolve/pallas_call | solution.py:310
  70.9 3.6 %all-to-all-start.1 = ((bf16[8,2,128,256]{3,2,1,0:T(8,128)(2,1)}), bf16[8,2,128,256]{3,2,1,0:T(8,128)(2,1)S(1)}, u32[]{:S(2)}, u32[]{:S(2)}) async-start(bf16[8,2,128,256]{3,2,1,0:T(8,128)(2,1)} %copy-done.10), calls=%async_computation.1 | async-start | bytes 2097152 | tf_op jit(solution)/shard_map/all_to_all | solution.py:483
  74.5 1.2 %copy-done.9 = bf16[512,1024]{1,0:T(8,128)(2,1)S(1)} copy-done((bf16[512,1024]{1,0:T(8,128)(2,1)S(1)}, bf16[512,1024]{1,0:T(8,128)(2,1)}, u32[]{:S(2)}) %copy-start.9) | copy-done | bytes 1048600
  77.4 1.2 %copy-done.20 = bf16[1024,512]{1,0:T(8,128)(2,1)S(1)} copy-done((bf16[1024,512]{1,0:T(8,128)(2,1)S(1)}, bf16[1024,512]{1,0:T(8,128)(2,1)}, u32[]{:S(2)}) %copy-start.20) | copy-done | bytes 1048600
  78.6 4.8 %correlate.1 = (f32[16,2048]{1,0:T(8,128)S(1)}, bf16[16,2048]{1,0:T(8,128)(2,1)S(1)}, bf16[16,2048]{1,0:T(8,128)(2,1)S(1)}) custom-call(bf16[16,128,256]{2,1,0:T(8,128)(2,1)} %all-to-all-done.refs_0_, bf16[128,256]{1,0:T(8,128)(2,1)S(1)} %bitcast.12, bf16[128,256]{1,0:T(8,128)(2,1)S(1)} %collective-permute-done.refs_2_, ...), custom_call_target="tpu_custom_call" | custom-call | flops 1888485376 | bytes 2097152 | tf_op jit(solution)/shard_map/correlate/pallas_call | solution.py:423
  84.0 1.3 %collective-permute-start.12 = (bf16[16,2048]{1,0:T(8,128)(2,1)S(1)}, bf16[16,2048]{1,0:T(8,128)(2,1)S(1)}, u32[]{:S(2)}, u32[]{:S(2)}) collective-permute-start(bf16[16,2048]{1,0:T(8,128)(2,1)S(1)} %get-tuple-element.34), channel_id=1, source_target_pairs={{16,8},{17,9},{18,10},{19,11},{20,12},{21,13},{22,14},{23,15},{24,... | collective-permute-start | bytes 196616 | tf_op jit(solution)/shard_map/ppermute | solution.py:491
  85.2 2.6 %collective-permute-start.11 = (bf16[16,2048]{1,0:T(8,128)(2,1)S(1)}, bf16[16,2048]{1,0:T(8,128)(2,1)S(1)}, u32[]{:S(2)}, u32[]{:S(2)}) collective-permute-start(bf16[16,2048]{1,0:T(8,128)(2,1)S(1)} %get-tuple-element.34), channel_id=1, source_target_pairs={{0,8},{1,9},{2,10},{3,11},{4,12},{5,13},{6,14},{7,15},{8,0},{9,1},... | collective-permute-start | bytes 196616 | tf_op jit(solution)/shard_map/ppermute | solution.py:490
  87.9 5.4 %collective-permute-done.12 = bf16[16,2048]{1,0:T(8,128)(2,1)S(1)} collective-permute-done((bf16[16,2048]{1,0:T(8,128)(2,1)S(1)}, bf16[16,2048]{1,0:T(8,128)(2,1)S(1)}, u32[]{:S(2)}, u32[]{:S(2)}) %collective-permute-start.12) | collective-permute-done | bytes 65568 | tf_op jit(solution)/shard_map/ppermute | solution.py:491
  94.4 1.6 %finish.1 = (bf16[1024,256]{1,0:T(8,128)(2,1)}, bf16[1024,256]{1,0:T(8,128)(2,1)}, bf16[1024,256]{1,0:T(8,128)(2,1)}, bf16[1024,256]{1,0:T(8,128)(2,1)}) custom-call(bf16[8,2,4,2,16,256]{5,4,3,2,1,0:T(8,128)(2,1)S(1)} %bitcast.10, bf16[1024,256]{1,0:T(8,128)(2,1)S(1)} %copy-done.1, bf16[1024,256]{1,0:T(8,128)(2,1)S(1)} %copy-done.3, ...), custom_call_target="tpu_custom_call" | custom-call | tf_op jit(solution)/shard_map/finish/pallas_call | solution.py:152
  (58 shorter events, 10.6 us)
Async XLA Ops:
  4.8 10.1 %copy-start.21 = (f32[16,2048]{1,0:T(8,128)S(1)}, f32[16,2048]{1,0:T(8,128)}, u32[]{:S(2)}) copy-start(f32[16,2048]{1,0:T(8,128)} %param.10) | copy-start | bytes 393220
  7.3 12.1 %copy-start.1 = (bf16[1024,256]{1,0:T(8,128)(2,1)S(1)}, bf16[1024,256]{1,0:T(8,128)(2,1)}, u32[]{:S(2)}) copy-start(bf16[1024,256]{1,0:T(8,128)(2,1)} %refs_1_.5) | copy-start | bytes 1572868
  7.3 12.1 %copy-start.3 = (bf16[1024,256]{1,0:T(8,128)(2,1)S(1)}, bf16[1024,256]{1,0:T(8,128)(2,1)}, u32[]{:S(2)}) copy-start(bf16[1024,256]{1,0:T(8,128)(2,1)} %refs_2_.5) | copy-start | bytes 1572868
  7.3 12.1 %copy-start.5 = (bf16[1024,256]{1,0:T(8,128)(2,1)S(1)}, bf16[1024,256]{1,0:T(8,128)(2,1)}, u32[]{:S(2)}) copy-start(bf16[1024,256]{1,0:T(8,128)(2,1)} %refs_3_.5) | copy-start | bytes 1572868
  7.3 12.1 %copy-start.7 = (bf16[1024,256]{1,0:T(8,128)(2,1)S(1)}, bf16[1024,256]{1,0:T(8,128)(2,1)}, u32[]{:S(2)}) copy-start(bf16[1024,256]{1,0:T(8,128)(2,1)} %refs_4_.2) | copy-start | bytes 1572868
  7.3 49.9 %all-to-all-start = ((bf16[16,128,256]{2,1,0:T(8,128)(2,1)}), bf16[16,128,256]{2,1,0:T(8,128)(2,1)}, u32[]{:S(2)}, u32[]{:S(2)}) async-start(bf16[16,128,256]{2,1,0:T(8,128)(2,1)} %bitcast), calls=%async_computation | async-start | bytes 2097152 | tf_op jit(solution)/shard_map/all_to_all | solution.py:463
  15.0 36.7 %copy-start.8 = (bf16[512,1024]{1,0:T(8,128)(2,1)S(1)}, bf16[512,1024]{1,0:T(8,128)(2,1)}, u32[]{:S(2)}) copy-start(bf16[512,1024]{1,0:T(8,128)(2,1)} %constant.4.clone.refs_4_.refs_10_.refs_9_) | copy-start | bytes 3145732
  15.0 32.1 %collective-permute-start.9 = (bf16[16,2048]{1,0:T(8,128)(2,1)S(1)}, bf16[16,2048]{1,0:T(8,128)(2,1)S(1)}, u32[]{:S(2)}, u32[]{:S(2)}) collective-permute-start(bf16[16,2048]{1,0:T(8,128)(2,1)S(1)} %convert_element_type.12.refs_0_), channel_id=1, source_target_pairs={{0,24},{1,25},{2,26},{3,27},{4,28},{5,29},{6,30},{7,31},{8,16},{9,... | collective-permute-start | bytes 196616 | tf_op jit(solution)/shard_map/ppermute | solution.py:474
  18.7 28.6 %collective-permute-start.8 = (bf16[16,2048]{1,0:T(8,128)(2,1)S(1)}, bf16[16,2048]{1,0:T(8,128)(2,1)S(1)}, u32[]{:S(2)}, u32[]{:S(2)}) collective-permute-start(bf16[16,2048]{1,0:T(8,128)(2,1)S(1)} %convert_element_type.12.refs_0_), channel_id=1, source_target_pairs={{0,8},{1,9},{2,10},{3,11},{4,12},{5,13},{6,14},{7,15},{8,0},{9,1},... | collective-permute-start | bytes 196616 | tf_op jit(solution)/shard_map/ppermute | solution.py:460
  18.9 28.4 %collective-permute-start.7 = (bf16[16,2048]{1,0:T(8,128)(2,1)S(1)}, bf16[16,2048]{1,0:T(8,128)(2,1)S(1)}, u32[]{:S(2)}, u32[]{:S(2)}) collective-permute-start(bf16[16,2048]{1,0:T(8,128)(2,1)S(1)} %convert_element_type.12.refs_0_), channel_id=1, source_target_pairs={{0,16},{16,0},{1,17},{17,1},{2,18},{18,2},{3,19},{19,3},{4,20},{20... | collective-permute-start | bytes 196616 | tf_op jit(solution)/shard_map/ppermute | solution.py:472
  21.8 28.2 %collective-permute-start = (bf16[128,256]{1,0:T(8,128)(2,1)S(1)}, bf16[128,256]{1,0:T(8,128)(2,1)S(1)}, u32[]{:S(2)}, u32[]{:S(2)}) collective-permute-start(bf16[128,256]{1,0:T(8,128)(2,1)S(1)} %bitcast.19), channel_id=1, source_target_pairs={{0,1},{1,0},{2,3},{3,2},{4,5},{5,4},{6,7},{7,6},{8,9},{9,8},{10,11... | collective-permute-start | bytes 196616 | tf_op jit(solution)/shard_map/ppermute | solution.py:460
  21.9 28.5 %collective-permute-start.1 = (bf16[128,256]{1,0:T(8,128)(2,1)S(1)}, bf16[128,256]{1,0:T(8,128)(2,1)S(1)}, u32[]{:S(2)}, u32[]{:S(2)}) collective-permute-start(bf16[128,256]{1,0:T(8,128)(2,1)S(1)} %bitcast.18), channel_id=1, source_target_pairs={{0,2},{1,3},{2,0},{3,1},{4,6},{5,7},{6,4},{7,5},{8,10},{9,11},{10,... | collective-permute-start | bytes 196616 | tf_op jit(solution)/shard_map/ppermute | solution.py:460
  47.0 6.1 %collective-permute-start.2 = (bf16[128,256]{1,0:T(8,128)(2,1)S(1)}, bf16[128,256]{1,0:T(8,128)(2,1)S(1)}, u32[]{:S(2)}, u32[]{:S(2)}) collective-permute-start(bf16[128,256]{1,0:T(8,128)(2,1)S(1)} %bitcast.17), channel_id=1, source_target_pairs={{0,3},{1,2},{2,1},{3,0},{4,7},{5,6},{6,5},{7,4},{8,11},{9,10},{10,... | collective-permute-start | bytes 196616 | tf_op jit(solution)/shard_map/ppermute | solution.py:460
  47.3 5.9 %collective-permute-start.3 = (bf16[128,256]{1,0:T(8,128)(2,1)S(1)}, bf16[128,256]{1,0:T(8,128)(2,1)S(1)}, u32[]{:S(2)}, u32[]{:S(2)}) collective-permute-start(bf16[128,256]{1,0:T(8,128)(2,1)S(1)} %bitcast.16), channel_id=1, source_target_pairs={{0,4},{1,5},{2,6},{3,7},{4,0},{5,1},{6,2},{7,3},{8,12},{9,13},{10,... | collective-permute-start | bytes 196616 | tf_op jit(solution)/shard_map/ppermute | solution.py:460
  47.3 6.4 %collective-permute-start.4 = (bf16[128,256]{1,0:T(8,128)(2,1)S(1)}, bf16[128,256]{1,0:T(8,128)(2,1)S(1)}, u32[]{:S(2)}, u32[]{:S(2)}) collective-permute-start(bf16[128,256]{1,0:T(8,128)(2,1)S(1)} %bitcast.15), channel_id=1, source_target_pairs={{0,5},{1,4},{2,7},{3,6},{4,1},{5,0},{6,3},{7,2},{8,13},{9,12},{10,... | collective-permute-start | bytes 196616 | tf_op jit(solution)/shard_map/ppermute | solution.py:460
  50.0 5.9 %collective-permute-start.5 = (bf16[128,256]{1,0:T(8,128)(2,1)S(1)}, bf16[128,256]{1,0:T(8,128)(2,1)S(1)}, u32[]{:S(2)}, u32[]{:S(2)}) collective-permute-start(bf16[128,256]{1,0:T(8,128)(2,1)S(1)} %bitcast.14), channel_id=1, source_target_pairs={{0,6},{1,7},{2,4},{3,5},{4,2},{5,3},{6,0},{7,1},{8,14},{9,15},{10,... | collective-permute-start | bytes 196616 | tf_op jit(solution)/shard_map/ppermute | solution.py:460
  50.3 6.2 %collective-permute-start.6 = (bf16[128,256]{1,0:T(8,128)(2,1)S(1)}, bf16[128,256]{1,0:T(8,128)(2,1)S(1)}, u32[]{:S(2)}, u32[]{:S(2)}) collective-permute-start(bf16[128,256]{1,0:T(8,128)(2,1)S(1)} %bitcast.13), channel_id=1, source_target_pairs={{0,7},{1,6},{2,5},{3,4},{4,3},{5,2},{6,1},{7,0},{8,15},{9,14},{10,... | collective-permute-start | bytes 196616 | tf_op jit(solution)/shard_map/ppermute | solution.py:460
  57.2 1.2 %copy-start.12 = (f32[8,32,1024]{2,1,0:T(8,128)S(1)}, f32[8,32,1024]{2,1,0:T(8,128)}, u32[]{:S(2)}) copy-start(f32[8,32,1024]{2,1,0:T(8,128)} %copy-done.11) | copy-start | bytes 3145732
  60.1 1.2 %copy-start.19 = (bf16[1024,512]{1,0:T(8,128)(2,1)S(1)}, bf16[1024,512]{1,0:T(8,128)(2,1)}, u32[]{:S(2)}) copy-start(bf16[1024,512]{1,0:T(8,128)(2,1)} %constant.5.clone.refs_11_.refs_10_) | copy-start | bytes 3145732
  70.9 23.5 %all-to-all-start.1 = ((bf16[8,2,128,256]{3,2,1,0:T(8,128)(2,1)}), bf16[8,2,128,256]{3,2,1,0:T(8,128)(2,1)S(1)}, u32[]{:S(2)}, u32[]{:S(2)}) async-start(bf16[8,2,128,256]{3,2,1,0:T(8,128)(2,1)} %copy-done.10), calls=%async_computation.1 | async-start | bytes 2097152 | tf_op jit(solution)/shard_map/all_to_all | solution.py:483
  74.5 1.2 %copy-start.9 = (bf16[512,1024]{1,0:T(8,128)(2,1)S(1)}, bf16[512,1024]{1,0:T(8,128)(2,1)}, u32[]{:S(2)}) copy-start(bf16[512,1024]{1,0:T(8,128)(2,1)} %constant.4.clone.refs_4_.refs_10_.refs_9_) | copy-start | bytes 3145732
  83.5 4.5 %collective-permute-start.10 = (bf16[16,2048]{1,0:T(8,128)(2,1)S(1)}, bf16[16,2048]{1,0:T(8,128)(2,1)S(1)}, u32[]{:S(2)}, u32[]{:S(2)}) collective-permute-start(bf16[16,2048]{1,0:T(8,128)(2,1)S(1)} %get-tuple-element.33), channel_id=1, source_target_pairs={{0,16},{16,0},{1,17},{17,1},{2,18},{18,2},{3,19},{19,3},{4,20},{20... | collective-permute-start | bytes 196616 | tf_op jit(solution)/shard_map/ppermute | solution.py:489
  84.0 9.3 %collective-permute-start.12 = (bf16[16,2048]{1,0:T(8,128)(2,1)S(1)}, bf16[16,2048]{1,0:T(8,128)(2,1)S(1)}, u32[]{:S(2)}, u32[]{:S(2)}) collective-permute-start(bf16[16,2048]{1,0:T(8,128)(2,1)S(1)} %get-tuple-element.34), channel_id=1, source_target_pairs={{16,8},{17,9},{18,10},{19,11},{20,12},{21,13},{22,14},{23,15},{24,... | collective-permute-start | bytes 196616 | tf_op jit(solution)/shard_map/ppermute | solution.py:491
  85.2 8.5 %collective-permute-start.11 = (bf16[16,2048]{1,0:T(8,128)(2,1)S(1)}, bf16[16,2048]{1,0:T(8,128)(2,1)S(1)}, u32[]{:S(2)}, u32[]{:S(2)}) collective-permute-start(bf16[16,2048]{1,0:T(8,128)(2,1)S(1)} %get-tuple-element.34), channel_id=1, source_target_pairs={{0,8},{1,9},{2,10},{3,11},{4,12},{5,13},{6,14},{7,15},{8,0},{9,1},... | collective-permute-start | bytes 196616 | tf_op jit(solution)/shard_map/ppermute | solution.py:490
  (13 other events, 12.0 us)
